TPU v7x, 128 devices: a whole 4x4x4 slice. The times are simulated.
128 devices in a mesh: row: 16 (over x, z), col: 8 (over y, core).
Axes of the slice: x: 4, y: 4, z: 4, core: 2. Of those that a mesh axis runs over, the one named last changes fastest.
Arguments:
- pair_repr: bfloat16 [1536, 1536, 128], P('row', 'col'), may hold values from -6 to 6
- pair_gain: float32 [128], replicated, may hold values from 0.1 to 1.9
- proj_weight: bfloat16 [128, 16], replicated, may hold values from -0.5 to 0.5
- query_weight: bfloat16 [128, 16], replicated, may hold values from -0.5 to 0.5
- key_weight: bfloat16 [128, 16], replicated, may hold values from -0.5 to 0.5
- mlp_first: bfloat16 [16, 16], replicated, may hold values from -1.5 to 1.5
- mlp_second: bfloat16 [16, 16], replicated, may hold values from -1.5 to 1.5
- mlp_third: bfloat16 [16, 16], replicated, may hold values from -1.5 to 1.5
- atom_feats: bfloat16 [32768, 128], P(('row', 'col')), may hold values from -6 to 6
- token_counts: int32 [16, 96], P('row'), may hold values from 1 to 23, 2048 in all within a row
- key_start: int32 [1024], P(('row', 'col')), may hold values from -96 to 0, as said below
- pair_cotangent: bfloat16 [32768, 2048], P(('row', 'col')), may hold values from -6 to 6
Outputs:
- pair_grad: bfloat16 [1536, 1536, 128], P('row', 'col')
- atom_grad: bfloat16 [32768, 128], P(('row', 'col'))
- proj_grad: float32 [128, 16], replicated
Inputs may be any that keep to these rules, and one draw needn't show every extreme that they name: `token_counts`: each row of counts sums to 2048; each row's largest count is 23. `key_start`: every query block lies inside its key window.
All inputs are finite; a program needn't handle non-finite values.
Results may differ from a plain program's by a relative error of at most 0.0038.
Values may be sent and summed in bfloat16 or wider, within the bound.
A program may use at most 128 MiB of HBM per device.

v0:
```python
import jax
import jax.numpy as jnp
from jax import lax
from jax.sharding import PartitionSpec as P

QBLK = 32
KWIN = 128


def with_halo(cells, sides, width):
    for axis, dim in sides:
        count = lax.axis_size(axis)
        ends = count - 1
        head = lax.slice_in_dim(cells, 0, width, axis=dim)
        tail = lax.slice_in_dim(cells, cells.shape[dim] - width, cells.shape[dim], axis=dim)
        cells = jnp.concatenate(
            [
                lax.ppermute(tail, axis, [(i, (i + 1) % count) for i in range(ends)]),
                cells,
                lax.ppermute(head, axis, [((i + 1) % count, i) for i in range(ends)]),
            ],
            axis=dim,
        )
    return cells


def shifted(block, axis, distance):
    devices = range(lax.axis_size(axis))
    route = [(i - distance, i) for i in devices if i - distance in devices]
    return lax.ppermute(block, axis, route)


def silu_slope(values):
    sigma = jax.nn.sigmoid(values)
    return sigma * (1.0 + values * (1.0 - sigma))


def norm_rows(values, gain_vec):
    floats = values.astype(jnp.float32)
    centre = floats - jnp.mean(floats, axis=-1, keepdims=True)
    spread = jnp.mean(centre * centre, axis=-1, keepdims=True)
    inv_scale = lax.rsqrt(spread + 1e-05)
    hatted = centre * inv_scale
    normed = (hatted * gain_vec).astype(jnp.bfloat16)
    return (hatted, inv_scale, normed)


def norm_back(grad_normed, hatted, inv_scale, gain_vec):
    scaled = grad_normed * gain_vec
    first_mean = jnp.mean(scaled, axis=-1, keepdims=True)
    second_mean = jnp.mean(scaled * hatted, axis=-1, keepdims=True)
    return (inv_scale * (scaled - first_mean - hatted * second_mean)).astype(jnp.bfloat16)


def pair_backward(start, cotangent, first_w, second_w, third_w):
    top = lax.Precision.HIGHEST
    hidden_one = jnp.einsum("qkc,cd->qkd", jax.nn.silu(start), first_w, precision=top)
    hidden_two = jnp.einsum("qkc,cd->qkd", jax.nn.silu(hidden_one), second_w, precision=top)
    back_two = jnp.einsum("qkd,cd->qkc", cotangent, third_w, precision=top) * silu_slope(hidden_two)
    back_one = jnp.einsum("qkd,cd->qkc", back_two, second_w, precision=top) * silu_slope(hidden_one)
    back_zero = jnp.einsum("qkd,cd->qkc", back_one, first_w, precision=top) * silu_slope(start)
    return cotangent + back_zero


def shards(
    pair_repr,
    pair_gain,
    proj_weight,
    query_weight,
    key_weight,
    mlp_first,
    mlp_second,
    mlp_third,
    atom_feats,
    token_counts,
    key_start,
    pair_cotangent,
):
    top = lax.Precision.HIGHEST
    tok_rows, tok_cols, channels = pair_repr.shape
    own_atoms = atom_feats.shape[0]
    pair_width = proj_weight.shape[1]
    col_count = lax.axis_size("col")
    row_count = lax.axis_size("row")
    row_index = lax.axis_index("row")
    col_index = lax.axis_index("col")
    device_index = row_index * col_count + col_index
    band_width = 3 * tok_rows
    reach_len = KWIN - QBLK
    ext_len = own_atoms + 2 * reach_len
    all_atoms = own_atoms * col_count * row_count
    all_tokens = tok_cols * col_count
    band_start = (row_index - 1) * tok_rows
    hatted, inv_scale, normed = norm_rows(pair_repr, pair_gain)
    tile_proj = jnp.dot(
        normed.reshape(-1, channels), proj_weight, preferred_element_type=jnp.float32
    )
    tile_proj = tile_proj.astype(jnp.bfloat16).reshape(tok_rows, tok_cols * pair_width)
    gathered = lax.all_gather(tile_proj, "col", axis=1, tiled=True)
    padded = jnp.pad(gathered, ((0, 0), (tok_rows * pair_width, tok_rows * pair_width)))
    band_proj = lax.dynamic_slice_in_dim(
        padded, row_index * tok_rows * pair_width, band_width * pair_width, 1
    )
    band_cube = band_proj.reshape(tok_rows, band_width, pair_width)
    counts = token_counts[0]
    ends = jnp.cumsum(counts)
    atom_slot = jnp.arange(own_atoms, dtype=jnp.int32)
    atom_row = col_index * own_atoms + atom_slot
    tok_local = jnp.sum((ends[None, :] <= atom_row[:, None]).astype(jnp.int32), axis=1)
    tok_global = row_index * tok_rows + tok_local
    ext_tokens = with_halo(tok_global, ((("row", "col"), 0),), reach_len)
    ext_feats = with_halo(atom_feats, ((("row", "col"), 0),), reach_len)
    ext_global = device_index * own_atoms - reach_len + jnp.arange(ext_len, dtype=jnp.int32)
    ext_valid = ((ext_global >= 0) & (ext_global < all_atoms)).astype(jnp.float32)
    ext_slot = jnp.clip(ext_tokens - band_start, 0, band_width - 1)
    key_onehot = (ext_slot[:, None] == jnp.arange(band_width, dtype=jnp.int32)[None, :]).astype(
        jnp.bfloat16
    )
    query_onehot = (tok_local[:, None] == jnp.arange(tok_rows, dtype=jnp.int32)[None, :]).astype(
        jnp.bfloat16
    )
    activated = jax.nn.silu(ext_feats.astype(jnp.float32)).astype(jnp.bfloat16)
    query_terms = jnp.dot(
        activated[reach_len : reach_len + own_atoms],
        query_weight,
        preferred_element_type=jnp.float32,
    )
    key_terms = jnp.dot(activated, key_weight, preferred_element_type=jnp.float32)
    cot_all = pair_cotangent.reshape(own_atoms, KWIN, pair_width).astype(jnp.float32)
    first_w = mlp_first.astype(jnp.float32)
    second_w = mlp_second.astype(jnp.float32)
    third_w = mlp_third.astype(jnp.float32)
    band_acc = jnp.zeros((tok_rows, band_width, pair_width), jnp.float32)
    key_grad = jnp.zeros((ext_len, pair_width), jnp.float32)
    query_parts = []
    for block in range(own_atoms // QBLK):
        lower = block * QBLK
        window = lower + key_start[block] + reach_len
        query_hot = query_onehot[lower : lower + QBLK]
        key_hot = lax.dynamic_slice_in_dim(key_onehot, window, KWIN, 0)
        selected = jnp.einsum(
            "li,ijc->ljc", query_hot, band_cube, preferred_element_type=jnp.float32
        ).astype(jnp.bfloat16)
        zp_pairs = jnp.einsum("kj,ljc->lkc", key_hot, selected, preferred_element_type=jnp.float32)
        key_part = lax.dynamic_slice_in_dim(key_terms, window, KWIN, 0)
        valid_part = lax.dynamic_slice_in_dim(ext_valid, window, KWIN, 0)
        start = zp_pairs + query_terms[lower : lower + QBLK, None, :] + key_part[None, :, :]
        cotangent = cot_all[lower : lower + QBLK] * valid_part[None, :, None]
        back = pair_backward(start, cotangent, first_w, second_w, third_w)
        query_parts.append(jnp.sum(back, axis=1))
        summed_keys = lax.dynamic_slice_in_dim(key_grad, window, KWIN, 0) + jnp.sum(back, axis=0)
        key_grad = lax.dynamic_update_slice_in_dim(key_grad, summed_keys, window, 0)
        by_token = jnp.einsum("li,lkc->ikc", query_hot.astype(jnp.float32), back, precision=top)
        band_acc = band_acc + jnp.einsum(
            "kj,ikc->ijc", key_hot.astype(jnp.float32), by_token, precision=top
        )
    band_grad = band_acc.reshape(tok_rows, band_width * pair_width)
    query_grad = jnp.concatenate(query_parts, axis=0)
    from_right = shifted(key_grad[:reach_len], ("row", "col"), -1)
    from_left = shifted(key_grad[own_atoms + reach_len :], ("row", "col"), 1)
    key_own = key_grad[reach_len : reach_len + own_atoms]
    key_own = key_own + jnp.pad(from_left, ((0, own_atoms - reach_len), (0, 0)))
    key_own = key_own + jnp.pad(from_right, ((own_atoms - reach_len, 0), (0, 0)))
    atom_sum = jnp.dot(query_grad, query_weight.astype(jnp.float32).T, precision=top) + jnp.dot(
        key_own, key_weight.astype(jnp.float32).T, precision=top
    )
    atom_grad = (atom_sum * silu_slope(atom_feats.astype(jnp.float32))).astype(jnp.bfloat16)
    row_wide = jnp.zeros((tok_rows, (all_tokens + 2 * tok_rows) * pair_width), jnp.float32)
    row_wide = lax.dynamic_update_slice(
        row_wide, band_grad, (jnp.int32(0), row_index * tok_rows * pair_width)
    )
    row_grad = row_wide[:, tok_rows * pair_width : (tok_rows + all_tokens) * pair_width]
    tile_grad = lax.psum_scatter(row_grad, "col", scatter_dimension=1, tiled=True)
    tile_grad = tile_grad.reshape(tok_rows, tok_cols, pair_width)
    grad_normed = jnp.einsum(
        "ijc,dc->ijd", tile_grad, proj_weight.astype(jnp.float32), precision=top
    )
    pair_grad = norm_back(grad_normed, hatted, inv_scale, pair_gain)
    weight_part = jnp.dot(
        normed.reshape(-1, channels).T, tile_grad.reshape(-1, pair_width), precision=top
    )
    proj_grad = lax.psum(weight_part, ("row", "col"))
    return (pair_grad, atom_grad, proj_grad)


def solution(mesh):
    placed = (
        P("row", "col", None),
        P(),
        P(),
        P(),
        P(),
        P(),
        P(),
        P(),
        P(("row", "col"), None),
        P("row", None),
        P(("row", "col")),
        P(("row", "col"), None),
    )
    return jax.shard_map(
        shards,
        mesh=mesh,
        in_specs=placed,
        out_specs=(P("row", "col", None), P(("row", "col"), None), P()),
        check_vma=False,
    )
```

profile of v0, /device:TPU:0, one launch (start us, length us, event | category | flops | bytes accessed | tf_op | source)
XLA Modules:
  0.0 336.6 jit_solution(8186737030719697459)
XLA Ops:
  7.2 4.3 %convert_reduce_fusion = f32[96,192]{1,0:T(8,128)S(1)} fusion(bf16[96,192,128]{2,1,0:T(8,128)(2,1)} %param.12), kind=kLoop, calls=%fused_computation.2 | loop fusion | flops 4700160 | bytes 4792320 | tf_op jit(solution)/shard_map/reduce_sum | solution.py:40
  11.6 6.4 %fusion.10 = f32[96,192]{1,0:T(8,128)S(1)} fusion(bf16[96,192,128]{2,1,0:T(8,128)(2,1)S(1)} %copy-done.1, f32[96,192]{1,0:T(8,128)S(1)} %broadcast_multiply_fusion.2), kind=kLoop, calls=%fused_computation.13 | loop fusion | flops 9418752 | bytes 4866048 | tf_op jit(solution)/shard_map/reduce_sum | solution.py:41
  18.0 5.8 %fusion.5 = bf16[96,192,128]{2,1,0:T(8,128)(2,1)S(1)} fusion(bf16[96,192,128]{2,1,0:T(8,128)(2,1)S(1)} %copy-done.1, f32[128]{0:T(128)S(1)} %copy-done.18, f32[96,192]{1,0:T(8,128)S(1)} %add_rsqrt_fusion, f32[96,192]{1,0:T(8,128)S(1)} %broadcast_multiply_fusion.2), kind=kLoop, calls=%fused_computation.8 | loop fusion | flops 11796480 | bytes 9585152 | tf_op jit(solution)/shard_map/convert_element_type | solution.py:44
  23.9 2.1 copy-done.2
  26.0 1.3 convolution_convert_fusion
  27.4 3.2 copy.253
  30.6 9.8 %reshape.163 = bf16[96,3072]{1,0:T(8,128)(2,1)} reshape(bf16[18432,16]{1,0:T(8,128)(2,1)} %copy.253) | data formatting | bytes 1179648 | tf_op jit(solution)/shard_map/reshape | solution.py:98
  41.7 1.3 collective-permute-start
  43.0 1.3 collective-permute-start.1
  44.9 4.9 %collective-permute-start.2 = (bf16[96,128]{1,0:T(8,128)(2,1)}, bf16[96,128]{1,0:T(8,128)(2,1)S(1)}, u32[]{:S(2)}, u32[]{:S(2)}) collective-permute-start(bf16[96,128]{1,0:T(8,128)(2,1)} %get-tuple-element.29), channel_id=1, source_target_pairs={{0,1},{1,2},{2,3},{3,4},{4,5},{5,6},{6,7},{7,8},{8,9},{9,10},{10,1... | collective-permute-start | bytes 73736 | tf_op jit(solution)/shard_map/ppermute | solution.py:18
  49.8 1.8 collective-permute-start.3
  66.2 1.2 copy.252
  103.8 1.5 fusion.50
  105.3 1.5 fusion.48
  106.7 2.0 fusion.46
  108.7 1.5 fusion.44
  110.2 1.5 fusion.42
  111.7 1.5 fusion.40
  113.2 1.5 fusion.38
  114.7 2.1 add_bitcast_fusion
  116.9 2.1 copy.325
  120.9 4.9 %slice.221 = f32[96,24576]{0,1:T(8,128)} slice(f32[96,27648]{0,1:T(8,128)S(1)} %constant_dynamic-update-slice_fusion), slice={[0:96], [1536:26112]} | slice | bytes 18874368 | tf_op jit(solution)/shard_map/slice | solution.py:172
  129.1 4.0 %collective-permute-start.4 = (f32[96,16]{0,1:T(8,128)S(1)}, f32[96,16]{0,1:T(8,128)S(1)}, u32[]{:S(2)}, u32[]{:S(2)}) collective-permute-start(f32[96,16]{0,1:T(8,128)S(1)} %get-tuple-element.31), channel_id=1, source_target_pairs={{0,1},{1,2},{2,3},{3,4},{4,5},{5,6},{6,7},{7,8},{8,9},{9,10},{10,1... | collective-permute-start | bytes 18440 | tf_op jit(solution)/shard_map/ppermute | solution.py:30
  133.2 1.5 collective-permute-start.5
  135.0 2.4 collective-permute-done.5
  138.5 66.8 %reduce-scatter.2.cloned.1.call-done = f32[96,3072]{0,1:T(8,128)} async-done(((f32[96,24576]{0,1:T(8,128)}), f32[96,3072]{0,1:T(8,128)}) %reduce-scatter.2.cloned.1.call-update) | async-done | bytes 1179664 | tf_op jit(solution)/shard_map/reduce_scatter | solution.py:173
  205.3 3.8 %copy.326 = f32[96,192,16]{1,2,0:T(8,128)} copy(f32[96,192,16]{0,2,1:T(8,128)} %bitcast.293) | data formatting | bytes 2359296 | tf_op jit(solution)/shard_map/reshape | solution.py:174
  209.1 22.9 %multiply_reduce_fusion = (f32[96,192]{1,0:T(8,128)S(1)}, f32[96,192]{1,0:T(8,128)S(1)}, f32[96,192,128]{2,1,0:T(8,128)}) fusion(f32[128]{0:T(128)S(1)} %copy-done.18, f32[96,192]{1,0:T(8,128)S(1)} %add_rsqrt_fusion, f32[96,192]{1,0:T(8,128)S(1)} %broadcast_multiply_fusion.2, bf16[96,192,128]{2,1,0:T(8,128)(2,1)} %param.12, f32[96,192,16]{1,2,0:T(8,128)} %copy.326, ...), kind=kOutput, calls=%fused_computation.14 | convolution fusion | flops 469463040 | bytes 15634944 | tf_op jit(solution)/shard_map/ijc,dc->ijd/dot_general | solution.py:175
  232.5 5.4 %reshape_reshape.3 = f32[18432,16]{1,0:T(8,128)} reshape(f32[96,3072]{1,0:T(8,128)S(1)} %copy.335) | data formatting | bytes 2359296 | tf_op jit(solution)/shard_map/reshape;reshape | solution.py:180
  237.8 12.6 %fusion.284 = f32[128,16]{0,1:T(8,128)S(1)} fusion(bf16[18432,128]{1,0:T(8,128)(2,1)} %bitcast.291, f32[18432,16]{1,0:T(8,128)} %reshape_reshape.3), kind=kOutput, calls=%fused_computation.386 | convolution fusion | flops 452984832 | bytes 5906432 | tf_op jit(solution)/shard_map/dot_general | solution.py:179
  250.4 64.9 %psum.7 = f32[128,16]{0,1:T(8,128)} all-reduce(f32[128,16]{0,1:T(8,128)S(1)} %fusion.284), channel_id=1, replica_groups=mesh['row'=16,'col'=8] {'row','col'}, use_global_device_ids=true, to_apply=%region_23.24 | all-reduce | flops 2048 | bytes 16384 | tf_op jit(solution)/shard_map/psum | solution.py:182
  315.3 14.3 %fusion.9 = bf16[96,192,128]{2,1,0:T(8,128)(2,1)} fusion(bf16[96,192,128]{2,1,0:T(8,128)(2,1)} %param.12, f32[96,192,128]{2,1,0:T(8,128)} %get-tuple-element.67, f32[96,192]{1,0:T(8,128)S(1)} %get-tuple-element.76, f32[96,192]{1,0:T(8,128)S(1)} %get-tuple-element.77, f32[128]{0:T(128)S(1)} %copy-done.18, f32[96,192]{1,0:T(8,128)S(1)} %add_rsqrt_fusion, ...), kind=kLoop, calls=%fused_computation.12 | loop fusion | flops 21233664 | bytes 19169792 | tf_op jit(solution)/shard_map/convert_element_type | solution.py:52
  (211 shorter events, 48.7 us)
Async XLA Ops:
  7.2 18.8 %copy-start = (bf16[128,16]{0,1:T(8,128)(2,1)S(1)}, bf16[128,16]{0,1:T(8,128)(2,1)}, u32[]{:S(2)}) copy-start(bf16[128,16]{0,1:T(8,128)(2,1)} %param.14) | copy-start | bytes 12292
  7.2 10.8 %copy-start.18 = (f32[128]{0:T(128)S(1)}, f32[128]{0:T(128)}, u32[]{:S(2)}) copy-start(f32[128]{0:T(128)} %param.13) | copy-start | bytes 1540
  7.2 70.6 %all-gather.2.cloned.1.call-start = ((), (), s32[]{:S(2)}) async-start(), calls=%async_computation.1 | async-start | bytes 5308416 | tf_op jit(solution)/shard_map/all_gather | solution.py:99
  7.2 4.3 %copy-start.1 = (bf16[96,192,128]{2,1,0:T(8,128)(2,1)S(1)}, bf16[96,192,128]{2,1,0:T(8,128)(2,1)}, u32[]{:S(2)}) copy-start(bf16[96,192,128]{2,1,0:T(8,128)(2,1)} %param.12) | copy-start | bytes 14155780
  27.3 13.2 %copy-start.19 = (s32[1,96]{1,0:T(1,128)S(1)}, s32[1,96]{1,0:T(1,128)}, u32[]{:S(2)}) copy-start(s32[1,96]{1,0:T(1,128)} %param.21) | copy-start | bytes 1156
  27.3 16.9 %copy-start.14 = (bf16[256,128]{1,0:T(8,128)(2,1)S(1)}, bf16[256,128]{1,0:T(8,128)(2,1)}, u32[]{:S(2)}) copy-start(bf16[256,128]{1,0:T(8,128)(2,1)} %param.20) | copy-start | bytes 196612
  27.3 24.2 %copy-start.15 = (s32[8]{0:T(128)S(1)}, s32[8]{0:T(128)}, u32[]{:S(2)}) copy-start(s32[8]{0:T(128)} %param.22) | copy-start | bytes 100
  27.4 35.2 %copy-start.5 = (bf16[256,2048]{1,0:T(8,128)(2,1)S(1)}, bf16[256,2048]{1,0:T(8,128)(2,1)}, u32[]{:S(2)}) copy-start(bf16[256,2048]{1,0:T(8,128)(2,1)} %param.23) | copy-start | bytes 3145732
  40.5 164.8 %reduce-scatter.2.cloned.1.call-start = ((), (), s32[]{:S(2)}) async-start(), calls=%async_computation.2 | async-start | bytes 14155776 | tf_op jit(solution)/shard_map/reduce_scatter | solution.py:173
  41.7 34.4 %collective-permute-start = (s32[96]{0:T(128)}, s32[96]{0:T(128)S(1)}, u32[]{:S(2)}, u32[]{:S(2)}) collective-permute-start(s32[96]{0:T(128)} %get-tuple-element.57), channel_id=1, source_target_pairs={{0,1},{1,2},{2,3},{3,4},{4,5},{5,6},{6,7},{7,8},{8,9},{9,10},{10,1... | collective-permute-start | bytes 1160 | tf_op jit(solution)/shard_map/ppermute | solution.py:18
  43.0 33.1 %collective-permute-start.1 = (s32[96]{0:T(128)S(1)}, s32[96]{0:T(128)S(1)}, u32[]{:S(2)}, u32[]{:S(2)}) collective-permute-start(s32[96]{0:T(128)S(1)} %get-tuple-element.58), channel_id=1, source_target_pairs={{1,0},{2,1},{3,2},{4,3},{5,4},{6,5},{7,6},{8,7},{9,8},{10,9},{11,1... | collective-permute-start | bytes 1160 | tf_op jit(solution)/shard_map/ppermute | solution.py:20
  44.9 31.4 %collective-permute-start.2 = (bf16[96,128]{1,0:T(8,128)(2,1)}, bf16[96,128]{1,0:T(8,128)(2,1)S(1)}, u32[]{:S(2)}, u32[]{:S(2)}) collective-permute-start(bf16[96,128]{1,0:T(8,128)(2,1)} %get-tuple-element.29), channel_id=1, source_target_pairs={{0,1},{1,2},{2,3},{3,4},{4,5},{5,6},{6,7},{7,8},{8,9},{9,10},{10,1... | collective-permute-start | bytes 73736 | tf_op jit(solution)/shard_map/ppermute | solution.py:18
  49.8 26.5 %collective-permute-start.3 = (bf16[96,128]{1,0:T(8,128)(2,1)S(1)}, bf16[96,128]{1,0:T(8,128)(2,1)S(1)}, u32[]{:S(2)}, u32[]{:S(2)}) collective-permute-start(bf16[96,128]{1,0:T(8,128)(2,1)S(1)} %get-tuple-element.30), channel_id=1, source_target_pairs={{1,0},{2,1},{3,2},{4,3},{5,4},{6,5},{7,6},{8,7},{9,8},{10,9},{11,1... | collective-permute-start | bytes 73736 | tf_op jit(solution)/shard_map/ppermute | solution.py:20
  69.3 7.0 %copy-start.16 = (bf16[128,16]{0,1:T(8,128)(2,1)S(1)}, bf16[128,16]{0,1:T(8,128)(2,1)}, u32[]{:S(2)}) copy-start(bf16[128,16]{0,1:T(8,128)(2,1)} %param.15) | copy-start | bytes 12292
  69.3 7.9 %copy-start.17 = (bf16[128,16]{0,1:T(8,128)(2,1)S(1)}, bf16[128,16]{0,1:T(8,128)(2,1)}, u32[]{:S(2)}) copy-start(bf16[128,16]{0,1:T(8,128)(2,1)} %param.16) | copy-start | bytes 12292
  82.1 2.3 copy-start.11
  82.1 2.3 copy-start.25
  83.7 2.7 copy-start.13
  83.7 2.7 copy-start.24
  85.7 2.7 copy-start.12
  85.7 2.7 copy-start.23
  87.7 2.7 copy-start.10
  87.7 2.7 copy-start.22
  89.7 2.7 copy-start.9
  89.7 2.7 copy-start.21
  91.7 2.7 copy-start.8
  91.7 2.7 copy-start.20
  94.4 3.0 copy-start.7
  95.9 2.7 copy-start.6
  129.1 5.9 %collective-permute-start.4 = (f32[96,16]{0,1:T(8,128)S(1)}, f32[96,16]{0,1:T(8,128)S(1)}, u32[]{:S(2)}, u32[]{:S(2)}) collective-permute-start(f32[96,16]{0,1:T(8,128)S(1)} %get-tuple-element.31), channel_id=1, source_target_pairs={{0,1},{1,2},{2,3},{3,4},{4,5},{5,6},{6,7},{7,8},{8,9},{9,10},{10,1... | collective-permute-start | bytes 18440 | tf_op jit(solution)/shard_map/ppermute | solution.py:30
  133.2 4.3 %collective-permute-start.5 = (f32[96,16]{0,1:T(8,128)S(1)}, f32[96,16]{0,1:T(8,128)S(1)}, u32[]{:S(2)}, u32[]{:S(2)}) collective-permute-start(f32[96,16]{0,1:T(8,128)S(1)} %get-tuple-element.32), channel_id=1, source_target_pairs={{1,0},{2,1},{3,2},{4,3},{5,4},{6,5},{7,6},{8,7},{9,8},{10,9},{11,1... | collective-permute-start | bytes 18440 | tf_op jit(solution)/shard_map/ppermute | solution.py:30
  209.1 22.9 %copy-start.4 = (f32[96,3072]{0,1:T(8,128)S(1)}, f32[96,3072]{0,1:T(8,128)}, u32[]{:S(2)}) copy-start(f32[96,3072]{0,1:T(8,128)} %reduce-scatter.2.cloned.1.call-done) | copy-start | bytes 3538948
  (5 other events, 10.2 us)
Sparse Core Ops, SparseCore 0:
  40.6 37.1 all-gather.1
  125.9 79.3 reduce-scatter.1
where the time goes:
time: 343 us; the launch traced here: 337 us
  matrix products  73.4 us (21%)
  waiting for transfers between devices  69.6 us (20%)
  blocking collectives  64.9 us (19%)
  local copies, waits for them, and re-layouts  56 us (16%)
  other arithmetic  32.1 us (9%)
  between operations  25.8 us (8%)
  starting transfers between devices  14.8 us (4%)
    reduce_scatter x1, waiting for transfers between devices, shards(): lax.psum_scatter(row_grad, 'col', scatter_dimension=1, tiled=True)  66.8 us
    psum x1, blocking collectives, shards(): proj_grad = lax.psum(weight_part, ('row', 'col'))  64.9 us
    dot_general x1, matrix products, shards(): jnp.einsum('ijc,dc->ijd', tile_grad, proj_weight.astype(jnp.float32), pre...  22.9 us
    convert_element_type x1, other arithmetic, norm_back(): (inv_scale * (scaled - first_mean - hatted * second_mean)).astype(jnp.bfl...  14.3 us
    dot_general x8, matrix products, shards(): jnp.einsum('kj,ikc->ijc', key_hot.astype(jnp.float32), by_token, precisio...  13 us
    slice x17, local copies, waits for them, and re-layouts, shards(): cotangent = cot_all[lower:lower + QBLK] * valid_part[None, :, None]  12.6 us
    dot_general x1, matrix products, shards(): jnp.dot(normed.reshape(-1, channels).T, tile_grad.reshape(-1, pair_width)...  12.6 us
    reshape x1, local copies, waits for them, and re-layouts, shards(): tile_proj.astype(jnp.bfloat16).reshape(tok_rows, tok_cols * pair_width)  9.84 us
  transfers between devices with their start and end apart: 8, of which 3 were waited for; matrix products, arithmetic and copies ran while one was open for 7% of the time, Pallas kernels for 0%

commit v1 on v0

v1 whole, which is shorter than its diff:
```python
import jax
import jax.numpy as jnp
from jax import lax
from jax.experimental import pallas as pl
from jax.experimental.pallas import tpu as pltpu
from jax.sharding import PartitionSpec as P

F32 = jnp.float32
BF16 = jnp.bfloat16
MESH = pl.DeviceIdType.MESH

N_ROW = 16
N_COL = 8
TOK = 96
COLS = 192
CP = 128
CA = 16
QBLK = 32
KWIN = 128
MOST = 23
ATOMS = 256
ROW_ATOMS = 2048
SLACK = TOK * MOST - ROW_ATOMS
HALO = KWIN - QBLK
EXT = ATOMS + 2 * HALO
NBLK = ATOMS // QBLK
LANES = QBLK * CA
KEYS = 48
QTOK = 32
GROUPS = TOK // 8
VMEM_LIMIT = 56 * 1024 * 1024


def key_base(col):
    return 16 * ((11 * col - 5 + 16) // 16) - 16


def query_base(col):
    return jnp.minimum(8 * ((11 * col) // 8), TOK - QTOK)


def query_base_static(col):
    return min(8 * ((11 * col) // 8), TOK - QTOK)


def iota(shape, dim):
    return lax.broadcasted_iota(jnp.int32, shape, dim)


def dot(a, b):
    return jnp.dot(a, b, preferred_element_type=F32)


def dot_nt(a, b):
    return lax.dot_general(a, b, (((1,), (1,)), ((), ())), preferred_element_type=F32)


def dot_tn(a, b):
    return lax.dot_general(a, b, (((0,), (0,)), ((), ())), preferred_element_type=F32)


def split(x):
    high = x.astype(BF16)
    low = (x - high.astype(F32)).astype(BF16)
    return high, low


def dot_split(x, w):
    high, low = split(x)
    return dot(high, w) + dot(low, w)


def sigmoid(x):
    return 0.5 * jnp.tanh(0.5 * x) + 0.5


def mesh_place():
    row = lax.axis_index("row")
    col = lax.axis_index("col")
    return row, col


def normalise(block):
    floats = block.astype(F32)
    centre = floats - jnp.mean(floats, axis=-1, keepdims=True)
    spread = jnp.mean(centre * centre, axis=-1, keepdims=True)
    inv_scale = lax.rsqrt(spread + 1e-05)
    return centre * inv_scale, inv_scale


def channel_eye(rows):
    return ((iota((rows, CA), 0) & (CA - 1)) == iota((rows, CA), 1)).astype(F32).astype(BF16)


def spread_projection(proj):
    eye = channel_eye(CP)
    wide = dot_nt(proj, eye)
    lane = iota((CP, CP), 1) // CA
    return jnp.concatenate(
        [jnp.where(lane == i, wide, 0.0).astype(BF16) for i in range(8)], axis=0
    )


def spread_projection_t(proj):
    eye = channel_eye(CP)
    tall = dot_nt(eye, proj)
    row = iota((CP, CP), 0) // CA
    return jnp.concatenate(
        [jnp.where(row == i, tall, 0.0).astype(BF16) for i in range(8)], axis=1
    )


def window_column(group, odd):
    first = 16 * ((8 * group - 13 + 16) // 16) - 16
    return jnp.clip(first + TOK * odd, 0, COLS - KEYS)


def corner_place(odd):
    return 80 * odd, 176 * (1 - odd)


def owners(row, col):
    odd = row % 2
    half = row // 2
    is_main = col == half
    is_corner = jnp.where(odd == 0, col == half - 1, col == half + 1)
    return odd, is_main, is_corner


def project_kernel(pair_ref, gain_ref, proj_ref, zrow_ref, corner_ref, band, cband, sems, csem):
    row, col = mesh_place()
    odd, is_main, is_corner = owners(row, col)

    def window_copy(group):
        first = pl.multiple_of(window_column(group, odd), 16)
        return pltpu.make_async_copy(
            pair_ref.at[pl.ds(8 * group, 8), pl.ds(first, KEYS)], band.at[group], sems.at[group]
        )

    @pl.when(is_main)
    def _():
        for group in range(GROUPS):
            window_copy(group).start()
        zrow_ref[...] = jnp.zeros_like(zrow_ref)
        spread_w = spread_projection(proj_ref[...])
        gain = gain_ref[...]
        for group in range(GROUPS):
            window_copy(group).wait()
            hatted, _ = normalise(band[group])
            normed = (hatted * gain).astype(BF16)
            flat = jnp.concatenate([normed[i] for i in range(8)], axis=1)
            at = pl.multiple_of(window_column(group, odd) - TOK * odd + 16, 16)
            zrow_ref[pl.ds(at, KEYS), 128 * group : 128 * group + 128] = dot(
                flat, spread_w
            ).astype(BF16)

    @pl.when(is_corner)
    def _():
        first_row, first_col = corner_place(odd)
        copy = pltpu.make_async_copy(
            pair_ref.at[pl.ds(first_row, 16), pl.ds(pl.multiple_of(first_col, 16), 16)],
            cband,
            csem,
        )
        copy.start()
        spread_w = spread_projection(proj_ref[...])
        copy.wait()
        hatted, _ = normalise(cband[...])
        normed = (hatted * gain_ref[...]).astype(BF16)
        for part in range(2):
            flat = jnp.concatenate([normed[8 * part + i] for i in range(8)], axis=1)
            corner_ref[:, 128 * part : 128 * part + 128] = dot(flat, spread_w).astype(BF16)


def project_band(pair_repr, gain, proj):
    return pl.pallas_call(
        project_kernel,
        out_shape=(
            jax.ShapeDtypeStruct((128, TOK * CA), BF16),
            jax.ShapeDtypeStruct((16, 256), BF16),
        ),
        in_specs=[
            pl.BlockSpec(memory_space=pl.ANY),
            pl.BlockSpec(memory_space=pltpu.VMEM),
            pl.BlockSpec(memory_space=pltpu.VMEM),
        ],
        out_specs=(
            pl.BlockSpec(memory_space=pltpu.VMEM),
            pl.BlockSpec(memory_space=pltpu.VMEM),
        ),
        scratch_shapes=[
            pltpu.VMEM((GROUPS, 8, KEYS, CP), BF16),
            pltpu.VMEM((16, 16, CP), BF16),
            pltpu.SemaphoreType.DMA((GROUPS,)),
            pltpu.SemaphoreType.DMA,
        ],
        compiler_params=pltpu.CompilerParams(vmem_limit_bytes=VMEM_LIMIT),
        name="project_band",
    )(pair_repr, gain, proj)


def neighbours(row, col):
    ahead = (
        jnp.where(col == N_COL - 1, lax.rem(row + 1, N_ROW), row),
        lax.rem(col + 1, N_COL),
    )
    behind = (
        jnp.where(col == 0, lax.rem(row + N_ROW - 1, N_ROW), row),
        lax.rem(col + N_COL - 1, N_COL),
    )
    return ahead, behind


def greet_row_and_neighbours(row, col):
    barrier = pltpu.get_barrier_semaphore()
    ahead, behind = neighbours(row, col)
    for step in range(1, N_COL):
        pl.semaphore_signal(
            barrier, inc=1, device_id=(row, lax.rem(col + step, N_COL)), device_id_type=MESH
        )

    @pl.when(col == 0)
    def _():
        pl.semaphore_signal(barrier, inc=1, device_id=behind, device_id_type=MESH)

    @pl.when(col == N_COL - 1)
    def _():
        pl.semaphore_signal(barrier, inc=1, device_id=ahead, device_id_type=MESH)

    extra = jnp.where(col == 0, 1, 0) + jnp.where(col == N_COL - 1, 1, 0)
    pl.semaphore_wait(barrier, N_COL - 1 + extra)
    return ahead, behind


def scatter_kernel(
    zrow_ref,
    corner_ref,
    feats_ref,
    counts_ref,
    patch_ref,
    patch_corner_ref,
    feats_before_ref,
    feats_after_ref,
    counts_before_ref,
    counts_after_ref,
    send_z,
    recv_z,
    send_c,
    recv_c,
    send_h,
    recv_h,
    local_sem,
):
    row, col = mesh_place()
    odd, is_main, is_corner = owners(row, col)
    half = row // 2
    ahead, behind = greet_row_and_neighbours(row, col)

    def z_part(target):
        base = key_base(target)
        return zrow_ref.at[
            pl.ds(base + 16, KEYS),
            pl.ds(query_base_static(target) * CA, QTOK * CA),
        ]

    def z_copy(target):
        return pltpu.make_async_remote_copy(
            src_ref=z_part(target),
            dst_ref=patch_ref,
            send_sem=send_z.at[target],
            recv_sem=recv_z,
            device_id=(row, target),
            device_id_type=MESH,
        )

    def z_local(target):
        return pltpu.make_async_copy(z_part(target), patch_ref, local_sem.at[0])

    corner_target = jnp.where(odd == 0, 0, N_COL - 1)

    def corner_copy():
        return pltpu.make_async_remote_copy(
            src_ref=corner_ref,
            dst_ref=patch_corner_ref,
            send_sem=send_c,
            recv_sem=recv_c,
            device_id=(row, corner_target),
            device_id_type=MESH,
        )

    corner_local = pltpu.make_async_copy(corner_ref, patch_corner_ref, local_sem.at[1])

    @pl.when(is_main)
    def _():
        for target in range(N_COL):

            @pl.when(col != target)
            def _():
                z_copy(target).start()

            @pl.when(col == target)
            def _():
                z_local(target).start()

    @pl.when(is_corner & (col != corner_target))
    def _():
        corner_copy().start()

    @pl.when(is_corner & (col == corner_target))
    def _():
        corner_local.start()

    halos = []
    for at, (src, dst, device) in enumerate(
        (
            (feats_ref.at[pl.ds(ATOMS - HALO, HALO)], feats_before_ref, ahead),
            (feats_ref.at[pl.ds(0, HALO)], feats_after_ref, behind),
            (counts_ref, counts_before_ref, ahead),
            (counts_ref, counts_after_ref, behind),
        )
    ):
        copy = pltpu.make_async_remote_copy(
            src_ref=src,
            dst_ref=dst,
            send_sem=send_h.at[at],
            recv_sem=recv_h.at[at],
            device_id=device,
            device_id_type=MESH,
        )
        copy.start()
        halos.append(copy)

    for copy in halos:
        copy.wait()

    @pl.when(is_main)
    def _():
        for target in range(N_COL):

            @pl.when(col != target)
            def _():
                z_copy(target).wait_send()

            @pl.when(col == target)
            def _():
                z_local(target).wait()

    @pl.when(jnp.logical_not(is_main))
    def _():
        z_copy(0).wait_recv()

    @pl.when(is_corner & (col != corner_target))
    def _():
        corner_copy().wait_send()

    @pl.when(is_corner & (col == corner_target))
    def _():
        corner_local.wait()

    owner = jnp.where(odd == 0, half - 1, half + 1)
    has_corner = (owner >= 0) & (owner < N_COL) & (owner != corner_target)

    @pl.when((col == corner_target) & has_corner)
    def _():
        corner_copy().wait_recv()


def scatter_band(zrow, corner, feats, counts):
    any_spec = pl.BlockSpec(memory_space=pl.ANY)
    return pl.pallas_call(
        scatter_kernel,
        out_shape=(
            jax.ShapeDtypeStruct((KEYS, QTOK * CA), BF16),
            jax.ShapeDtypeStruct((16, 256), BF16),
            jax.ShapeDtypeStruct((HALO, CP), BF16),
            jax.ShapeDtypeStruct((HALO, CP), BF16),
            jax.ShapeDtypeStruct((1, TOK), jnp.int32),
            jax.ShapeDtypeStruct((1, TOK), jnp.int32),
        ),
        in_specs=[any_spec] * 4,
        out_specs=(any_spec,) * 6,
        scratch_shapes=[
            pltpu.SemaphoreType.DMA((N_COL,)),
            pltpu.SemaphoreType.DMA,
            pltpu.SemaphoreType.DMA,
            pltpu.SemaphoreType.DMA,
            pltpu.SemaphoreType.DMA((4,)),
            pltpu.SemaphoreType.DMA((4,)),
            pltpu.SemaphoreType.DMA((2,)),
        ],
        compiler_params=pltpu.CompilerParams(
            collective_id=0, has_side_effects=True, vmem_limit_bytes=VMEM_LIMIT
        ),
        name="scatter_band",
    )(zrow, corner, feats, counts)


def swap_atoms(block):
    row = iota((8, 128), 0)
    lane = iota((8, 128), 1)
    turn = (lane + CA * row) % 128
    pick = (row + 8 - lane // CA) % 8
    pieces = []
    for at in range(block.shape[0] // 8):
        piece = jnp.take_along_axis(block[8 * at : 8 * at + 8], turn, axis=1)
        piece = jnp.take_along_axis(piece, pick, axis=0)
        pieces.append(jnp.take_along_axis(piece, turn, axis=1))
    return pieces


def pair_kernel(
    start_ref,
    cot_ref,
    feats_ref,
    feats_before_ref,
    feats_after_ref,
    counts_ref,
    counts_before_ref,
    counts_after_ref,
    patch_ref,
    patch_corner_ref,
    query_w_ref,
    key_w_ref,
    first_w_ref,
    second_w_ref,
    third_w_ref,
    key_out_ref,
    query_out_ref,
    token_out_ref,
    blank_ref,
    act_ext,
    lhs,
    rhs,
    query_high,
    query_low,
    cot,
    state,
    mixers,
    key_tiled,
    query_tiled,
    slot_from,
    slot_to,
    hot_ref,
    zeros,
    zero_sem,
):
    row, col = mesh_place()
    odd = row % 2
    zeros[...] = jnp.zeros_like(zeros)
    fills = [
        pltpu.make_async_copy(zeros, blank_ref.at[pl.ds(8 * g, 8)], zero_sem.at[g])
        for g in range(GROUPS)
    ]
    for fill in fills:
        fill.start()

    eye = channel_eye(LANES)
    eye16 = eye[:256]
    same = (iota((256, 256), 0) // CA) == (iota((256, 256), 1) // CA)

    def mixer(weight, flip):
        left = dot_nt(eye16, weight) if flip else dot(eye16, weight)
        wide = dot_nt(left.astype(BF16), eye16)
        return jnp.where(same, wide, 0.0).astype(BF16)

    mixers[0] = mixer(first_w_ref[...], False)
    mixers[1] = mixer(second_w_ref[...], False)
    mixers[2] = mixer(third_w_ref[...], True)
    mixers[3] = mixer(second_w_ref[...], True)
    mixers[4] = mixer(first_w_ref[...], True)
    key_tiled[...] = dot_nt(eye, key_w_ref[...]).astype(BF16)
    query_tiled[...] = dot_nt(eye, query_w_ref[...]).astype(BF16)
    rhs[128:256, :] = dot_nt(key_w_ref[...], eye).astype(BF16)
    rhs[112:128, :] = jnp.zeros((16, LANES), BF16)

    def activate(feats):
        floats = feats.astype(F32)
        return floats * jax.nn.sigmoid(floats)

    own_act = activate(feats_ref[...]).astype(BF16)
    act_ext[0:HALO] = activate(feats_before_ref[...])
    act_ext[HALO : HALO + ATOMS] = activate(feats_ref[...])
    act_ext[HALO + ATOMS : EXT] = activate(feats_after_ref[...])

    lane_index = iota((QBLK, LANES), 1)
    lane_atom = 8 * (lane_index // 128) + ((8 - (lane_index % 128) // CA) % 8)
    lane_is_row = lane_atom == iota((QBLK, LANES), 0)
    query_wide = dot_nt(query_w_ref[...], eye).astype(BF16)
    for block in range(NBLK):
        terms = dot(own_act[QBLK * block : QBLK * block + QBLK], query_wide)
        high, low = split(jnp.where(lane_is_row, terms, 0.0))
        query_high[QBLK * block : QBLK * block + QBLK] = high
        query_low[QBLK * block : QBLK * block + QBLK] = low

    base = key_base(col)
    own = counts_ref[...].astype(F32)
    before = counts_before_ref[...].astype(F32)
    after = counts_after_ref[...].astype(F32)

    def rows_of(counts, rows):
        return jnp.broadcast_to(counts, (rows, TOK)).astype(BF16)

    def as_mask(flag):
        return jnp.where(flag, 1.0, 0.0).astype(BF16)

    def lane_bounds(offset):
        token = iota((TOK, 128), 1) + (base + offset)
        index = iota((TOK, 128), 0)
        total = dot(rows_of(own, 8), as_mask(index < token))
        total += dot(rows_of(after, 8), as_mask(index + TOK < token))
        return total - dot(rows_of(before, 8), as_mask(index - TOK >= token))

    def column_bounds(offset):
        token = iota((KEYS, TOK), 0) + (base + offset)
        index = iota((KEYS, TOK), 1)
        total = dot_nt(as_mask(index < token), rows_of(own, 128))
        total += dot_nt(as_mask(index + TOK < token), rows_of(after, 128))
        return total - dot_nt(as_mask(index - TOK >= token), rows_of(before, 128))

    lane = iota((8, 128), 1)
    far = 1.0e6
    lane_from = jnp.where(lane < 48, lane_bounds(0), jnp.where(lane < 112, -far, far))[0:1]
    lane_to = jnp.where(lane < 48, lane_bounds(1), jnp.where(lane < 112, far, -far))[0:1]
    column_from = column_bounds(0)
    column_to = column_bounds(1)

    first_query = query_base(col)
    slot = iota((LANES, TOK), 0) // CA + first_query
    slot_index = iota((LANES, TOK), 1)
    own_rows = rows_of(own, 128)
    slot_from[...] = dot_nt(as_mask(slot_index < slot), own_rows)
    slot_to[...] = dot_nt(as_mask(slot_index < slot + 1), own_rows)

    def swap_step(chunk, carry):
        at = pl.multiple_of(128 * chunk, 128)
        turned = swap_atoms(cot_ref[:, pl.ds(at, 128)].astype(F32))
        for block in range(NBLK):
            to = pl.multiple_of(128 * block + 8 * chunk, 8)
            for part in range(4):
                cot[pl.ds(to, 8), 128 * part : 128 * part + 128] = turned[4 * block + part]
        return carry

    lax.fori_loop(0, ATOMS * 8 // 128, swap_step, 0)

    has_before = (col == 0) & (odd == 0) & (row > 0)
    has_after = (col == N_COL - 1) & (odd == 1) & (row < N_ROW - 1)
    patch = patch_ref[...]
    corner = patch_corner_ref[...]
    head = jnp.where(has_before, corner, patch[0:16, 0:256])
    tail = jnp.where(has_after, corner, patch[32:48, 256:512])
    patch_ref[0:16, 0:256] = head
    patch_ref[32:48, 256:512] = tail

    lane_atom_row = (
        8 * (iota((1, LANES), 1) // 128) + ((8 - (iota((1, LANES), 1) % 128) // CA) % 8)
    ).astype(F32)
    channel_match = (iota((256, 128), 0) % CA) == (iota((256, 128), 1) % CA)

    def block_place(block):
        first = col * ATOMS + block * QBLK
        token = 8 * (first // (8 * MOST)) - first_query
        return first, pl.multiple_of(token * CA, 128)

    def query_hot(block):
        first, at = block_place(block)
        low = slot_from[pl.ds(at, 256), :]
        high = slot_to[pl.ds(at, 256), :]
        parts = []
        for part in range(4):
            atom = lane_atom_row[:, 128 * part : 128 * part + 128] + first.astype(F32)
            hot = (low <= atom) & (atom < high) & channel_match
            parts.append(jnp.where(hot, 1.0, 0.0).astype(BF16))
        return jnp.concatenate(parts, axis=1)

    def key_first(block):
        return col * ATOMS + block * QBLK + start_ref[block]

    def start_step(block, carry):
        _, at = block_place(block)
        hot = query_hot(block)
        hot_ref[block] = hot
        window = start_ref[block] + block * QBLK + HALO
        atom = (iota((KWIN, 128), 0) + key_first(block)).astype(F32)
        lhs[:, 0:128] = as_mask((lane_from <= atom) & (atom < lane_to))
        lhs[:, 128:256] = act_ext[pl.ds(window, KWIN), :].astype(BF16)
        rhs[0:48, :] = dot(patch_ref[:, pl.ds(at, 256)], hot).astype(BF16)
        mine = pl.multiple_of(block * QBLK, QBLK)
        rhs[48:80, :] = query_high[pl.ds(mine, QBLK), :]
        rhs[80:112, :] = query_low[pl.ds(mine, QBLK), :]
        state[pl.ds(pl.multiple_of(block * KWIN, KWIN), KWIN), :] = dot(lhs[...], rhs[...])
        return carry

    lax.fori_loop(0, NBLK, start_step, 0)

    atom_low = jnp.where(row == 0, 0, -ROW_ATOMS)
    atom_high = jnp.where(row == N_ROW - 1, ROW_ATOMS, 2 * ROW_ATOMS)

    def slope(value, sigma, act):
        return sigma + act - act * sigma

    def mlp_step(step, carry):
        pair = step // 2
        at = pl.multiple_of(256 * pair, 256)
        place = pl.ds(at, 256), pl.ds(pl.multiple_of(256 * (step % 2), 256), 256)
        value = state[place]
        index = iota((256, 256), 0)
        begin = jnp.where(index < KWIN, key_first(2 * pair), key_first(2 * pair + 1) - KWIN)
        atom = index + begin
        grad = jnp.where((atom >= atom_low) & (atom < atom_high), cot[place], 0.0)
        sig_0 = sigmoid(value)
        act_0 = value * sig_0
        one = dot_split(act_0, mixers[0])
        sig_1 = sigmoid(one)
        act_1 = one * sig_1
        two = dot_split(act_1, mixers[1])
        sig_2 = sigmoid(two)
        back = dot(grad.astype(BF16), mixers[2]) * slope(two, sig_2, two * sig_2)
        back = dot_split(back, mixers[3]) * slope(one, sig_1, act_1)
        back = dot_split(back, mixers[4]) * slope(value, sig_0, act_0)
        state[place] = grad + back
        return carry

    lax.fori_loop(0, 8, mlp_step, 0)

    key_out_ref[...] = jnp.zeros_like(key_out_ref)
    token_out_ref[...] = jnp.zeros_like(token_out_ref)

    def sum_step(block, carry):
        _, at = block_place(block)
        window = start_ref[block] + block * QBLK + HALO
        back = state[pl.ds(pl.multiple_of(block * KWIN, KWIN), KWIN), :]
        high, low = split(back)
        key_out_ref[pl.ds(window, KWIN), :] += dot(high, key_tiled[...]) + dot(
            low, key_tiled[...]
        )
        over_keys = jnp.sum(back, axis=0, keepdims=True)
        over_keys = jnp.where(lane_is_row, over_keys, 0.0)
        mine = pl.multiple_of(block * QBLK, QBLK)
        query_out_ref[pl.ds(mine, QBLK), :] = dot_split(over_keys, query_tiled[...])
        atom = (iota((KEYS, 128), 1) + key_first(block)).astype(F32)
        key_hot = as_mask((column_from <= atom) & (atom < column_to))
        by_token = dot(key_hot, high) + dot(key_hot, low)
        high, low = split(by_token)
        hot = hot_ref[block]
        token_out_ref[:, pl.ds(at, 256)] += dot_nt(high, hot) + dot_nt(low, hot)
        return carry

    lax.fori_loop(0, NBLK, sum_step, 0)
    for fill in fills:
        fill.wait()


def atom_pairs(key_start, cot, feats, halo_feats, counts, halo_counts, patch, corner, weights):
    vmem = pl.BlockSpec(memory_space=pltpu.VMEM)
    return pl.pallas_call(
        pair_kernel,
        out_shape=(
            jax.ShapeDtypeStruct((EXT, CP), F32),
            jax.ShapeDtypeStruct((ATOMS, CP), F32),
            jax.ShapeDtypeStruct((KEYS, QTOK * CA), F32),
            jax.ShapeDtypeStruct((TOK, COLS, CP), BF16),
        ),
        in_specs=[pl.BlockSpec(memory_space=pltpu.SMEM)] + [vmem] * 14,
        out_specs=(vmem, vmem, vmem, pl.BlockSpec(memory_space=pl.ANY)),
        scratch_shapes=[
            pltpu.VMEM((EXT, CP), F32),
            pltpu.VMEM((KWIN, 256), BF16),
            pltpu.VMEM((256, LANES), BF16),
            pltpu.VMEM((ATOMS, LANES), BF16),
            pltpu.VMEM((ATOMS, LANES), BF16),
            pltpu.VMEM((NBLK * KWIN, LANES), F32),
            pltpu.VMEM((NBLK * KWIN, LANES), F32),
            pltpu.VMEM((5, 256, 256), BF16),
            pltpu.VMEM((LANES, CP), BF16),
            pltpu.VMEM((LANES, CP), BF16),
            pltpu.VMEM((LANES, 128), F32),
            pltpu.VMEM((LANES, 128), F32),
            pltpu.VMEM((NBLK, 256, LANES), BF16),
            pltpu.VMEM((8, COLS, CP), BF16),
            pltpu.SemaphoreType.DMA((GROUPS,)),
        ],
        compiler_params=pltpu.CompilerParams(vmem_limit_bytes=VMEM_LIMIT),
        name="atom_pairs",
    )(key_start, cot, feats, *halo_feats, counts, *halo_counts, patch, corner, *weights)


def gather_kernel(
    key_ref,
    token_ref,
    from_before_ref,
    from_after_ref,
    patches_ref,
    corner_ref,
    send_t,
    recv_t,
    send_c,
    recv_c,
    send_h,
    recv_h,
    local_sem,
):
    row, col = mesh_place()
    odd, is_main, is_corner = owners(row, col)
    half = row // 2
    ahead, behind = greet_row_and_neighbours(row, col)

    def token_copy(source):
        return pltpu.make_async_remote_copy(
            src_ref=token_ref,
            dst_ref=patches_ref.at[source],
            send_sem=send_t,
            recv_sem=recv_t.at[source],
            device_id=(row, half),
            device_id_type=MESH,
        )

    token_local = pltpu.make_async_copy(token_ref, patches_ref.at[col], local_sem.at[0])

    @pl.when(jnp.logical_not(is_main))
    def _():
        token_copy(col).start()

    @pl.when(is_main)
    def _():
        token_local.start()

    corner_source = jnp.where(odd == 0, 0, N_COL - 1)
    corner_owner = jnp.where(odd == 0, half - 1, half + 1)
    corner_exists = (corner_owner >= 0) & (corner_owner < N_COL)
    corner_part = token_ref.at[
        pl.ds(pl.multiple_of(32 * odd, 16), 16), pl.ds(pl.multiple_of(256 * odd, 256), 256)
    ]
    corner_copy = pltpu.make_async_remote_copy(
        src_ref=corner_part,
        dst_ref=corner_ref,
        send_sem=send_c,
        recv_sem=recv_c,
        device_id=(row, jnp.clip(corner_owner, 0, N_COL - 1)),
        device_id_type=MESH,
    )
    corner_local = pltpu.make_async_copy(corner_part, corner_ref, local_sem.at[1])
    corner_here = (col == corner_source) & corner_exists

    @pl.when(corner_here & (corner_owner != col))
    def _():
        corner_copy.start()

    @pl.when(corner_here & (corner_owner == col))
    def _():
        corner_local.start()

    halos = []
    for at, (src, dst, device) in enumerate(
        (
            (key_ref.at[pl.ds(HALO + ATOMS, HALO)], from_before_ref, ahead),
            (key_ref.at[pl.ds(0, HALO)], from_after_ref, behind),
        )
    ):
        copy = pltpu.make_async_remote_copy(
            src_ref=src,
            dst_ref=dst,
            send_sem=send_h.at[at],
            recv_sem=recv_h.at[at],
            device_id=device,
            device_id_type=MESH,
        )
        copy.start()
        halos.append(copy)
    for copy in halos:
        copy.wait()

    @pl.when(jnp.logical_not(is_main))
    def _():
        token_copy(col).wait_send()

    @pl.when(is_main)
    def _():
        token_local.wait()
        for source in range(N_COL):

            @pl.when(col != source)
            def _():
                token_copy(source).wait_recv()

    @pl.when(corner_here & (corner_owner != col))
    def _():
        corner_copy.wait_send()

    @pl.when(corner_here & (corner_owner == col))
    def _():
        corner_local.wait()

    @pl.when(is_corner & (col != corner_source))
    def _():
        corner_copy.wait_recv()


def gather_gradients(key_sums, token_sums):
    any_spec = pl.BlockSpec(memory_space=pl.ANY)
    return pl.pallas_call(
        gather_kernel,
        out_shape=(
            jax.ShapeDtypeStruct((HALO, CP), F32),
            jax.ShapeDtypeStruct((HALO, CP), F32),
            jax.ShapeDtypeStruct((N_COL, KEYS, QTOK * CA), F32),
            jax.ShapeDtypeStruct((16, 256), F32),
        ),
        in_specs=[any_spec] * 2,
        out_specs=(any_spec,) * 4,
        scratch_shapes=[
            pltpu.SemaphoreType.DMA,
            pltpu.SemaphoreType.DMA((N_COL,)),
            pltpu.SemaphoreType.DMA,
            pltpu.SemaphoreType.DMA,
            pltpu.SemaphoreType.DMA((2,)),
            pltpu.SemaphoreType.DMA((2,)),
            pltpu.SemaphoreType.DMA((2,)),
        ],
        compiler_params=pltpu.CompilerParams(
            collective_id=1, has_side_effects=True, vmem_limit_bytes=VMEM_LIMIT
        ),
        name="gather_gradients",
    )(key_sums, token_sums)


def finish_kernel(
    pair_ref,
    gain_ref,
    proj_ref,
    patches_ref,
    corner_ref,
    blank_ref,
    key_ref,
    from_before_ref,
    from_after_ref,
    query_ref,
    feats_ref,
    pair_grad_ref,
    atom_grad_ref,
    proj_grad_ref,
    band,
    grads,
    patches,
    tokens,
    weight_sum,
    sems,
    out_sems,
    patch_sems,
):
    row, col = mesh_place()
    odd, is_main, is_corner = owners(row, col)

    def in_place(group):
        first = pl.multiple_of(window_column(group, odd), 16)
        return pl.ds(8 * group, 8), pl.ds(first, KEYS)

    def window_copy(group):
        return pltpu.make_async_copy(
            pair_ref.at[in_place(group)], band.at[group], sems.at[group]
        )

    def out_copy(group):
        return pltpu.make_async_copy(
            grads.at[group], pair_grad_ref.at[in_place(group)], out_sems.at[group]
        )

    def patch_copy(source):
        return pltpu.make_async_copy(
            patches_ref.at[source], patches.at[source], patch_sems.at[source]
        )

    first_row, first_col = corner_place(odd)
    corner_at = pl.ds(first_row, 16), pl.ds(pl.multiple_of(first_col, 16), 16)
    half_band = band.at[0, :, pl.ds(0, 32)]

    @pl.when(is_main)
    def _():
        for group in range(GROUPS):
            window_copy(group).start()
        for source in range(N_COL):
            patch_copy(source).start()

    total = query_ref[...] + key_ref[HALO : HALO + ATOMS]
    lead = total[:HALO] + from_before_ref[...]
    trail = total[ATOMS - HALO :] + from_after_ref[...]
    total = jnp.concatenate([lead, total[HALO : ATOMS - HALO], trail], axis=0)
    floats = feats_ref[...].astype(F32)
    sigma = jax.nn.sigmoid(floats)
    atom_grad_ref[...] = (total * (sigma * (1.0 + floats * (1.0 - sigma)))).astype(BF16)

    weight_sum[...] = jnp.zeros_like(weight_sum)

    def gradient(normed_rows, hatted, inv_scale, token_part, spread_w, gain):
        high, low = split(token_part)
        wide = dot(high, spread_w) + dot(low, spread_w)
        scaled = jnp.stack([wide[:, 128 * i : 128 * i + 128] for i in range(8)]) * gain
        first_mean = jnp.mean(scaled, axis=-1, keepdims=True)
        second_mean = jnp.mean(scaled * hatted, axis=-1, keepdims=True)
        flat = jnp.concatenate([normed_rows[i] for i in range(8)], axis=1)
        weight_sum[...] += dot_tn(high, flat) + dot_tn(low, flat)
        return (inv_scale * (scaled - first_mean - hatted * second_mean)).astype(BF16)

    @pl.when(is_main)
    def _():
        spread_w = spread_projection_t(proj_ref[...])
        gain = gain_ref[...]
        tokens[...] = jnp.zeros_like(tokens)
        for source in range(N_COL):
            patch_copy(source).wait()
            at = key_base(source) + 16
            lanes = query_base_static(source) * CA
            tokens[at : at + KEYS, lanes : lanes + QTOK * CA] += patches[source]
        for group in range(GROUPS):
            window_copy(group).wait()
            hatted, inv_scale = normalise(band[group])
            normed = (hatted * gain).astype(BF16)
            at = pl.multiple_of(window_column(group, odd) - TOK * odd + 16, 16)
            part = tokens[pl.ds(at, KEYS), 128 * group : 128 * group + 128]
            grads[group] = gradient(normed, hatted, inv_scale, part, spread_w, gain)
            out_copy(group).start()
        for group in range(GROUPS):
            out_copy(group).wait()

    @pl.when(is_corner)
    def _():
        loads = [
            pltpu.make_async_copy(
                pair_ref.at[
                    pl.ds(first_row + 8 * part, 8), pl.ds(pl.multiple_of(first_col, 16), 16)
                ],
                band.at[part, :, pl.ds(0, 16)],
                sems.at[part],
            )
            for part in range(2)
        ]
        loads.append(
            pltpu.make_async_copy(
                corner_ref, tokens.at[pl.ds(0, 16), pl.ds(0, 256)], patch_sems.at[0]
            )
        )
        for load in loads:
            load.start()
        for load in loads:
            load.wait()
        spread_w = spread_projection_t(proj_ref[...])
        gain = gain_ref[...]
        stores = []
        for part in range(2):
            hatted, inv_scale = normalise(band[part, :, 0:16])
            normed = (hatted * gain).astype(BF16)
            tokens_part = tokens[0:16, 128 * part : 128 * part + 128]
            grads[part, :, 0:16] = gradient(
                normed, hatted, inv_scale, tokens_part, spread_w, gain
            )
            store = pltpu.make_async_copy(
                grads.at[part, :, pl.ds(0, 16)],
                pair_grad_ref.at[
                    pl.ds(first_row + 8 * part, 8), pl.ds(pl.multiple_of(first_col, 16), 16)
                ],
                out_sems.at[part],
            )
            store.start()
            stores.append(store)
        for store in stores:
            store.wait()

    result = jnp.zeros((CA, CP), F32)
    for i in range(8):
        result += weight_sum[CA * i : CA * i + CA, 128 * i : 128 * i + 128]
    proj_grad_ref[...] = result


def finish(pair_repr, gain, proj, patches, corner, blank, key_sums, halos, query_sums, feats):
    vmem = pl.BlockSpec(memory_space=pltpu.VMEM)
    any_spec = pl.BlockSpec(memory_space=pl.ANY)
    return pl.pallas_call(
        finish_kernel,
        out_shape=(
            jax.ShapeDtypeStruct((TOK, COLS, CP), BF16),
            jax.ShapeDtypeStruct((ATOMS, CP), BF16),
            jax.ShapeDtypeStruct((CA, CP), F32),
        ),
        in_specs=[any_spec, vmem, vmem, any_spec, any_spec, any_spec] + [vmem] * 5,
        out_specs=(any_spec, vmem, vmem),
        input_output_aliases={5: 0},
        scratch_shapes=[
            pltpu.VMEM((GROUPS, 8, KEYS, CP), BF16),
            pltpu.VMEM((GROUPS, 8, KEYS, CP), BF16),
            pltpu.VMEM((N_COL, KEYS, QTOK * CA), F32),
            pltpu.VMEM((128, TOK * CA), F32),
            pltpu.VMEM((128, 8 * CP), F32),
            pltpu.SemaphoreType.DMA((GROUPS,)),
            pltpu.SemaphoreType.DMA((GROUPS,)),
            pltpu.SemaphoreType.DMA((N_COL,)),
        ],
        compiler_params=pltpu.CompilerParams(vmem_limit_bytes=VMEM_LIMIT),
        name="finish",
    )(pair_repr, gain, proj, patches, corner, blank, key_sums, *halos, query_sums, feats)


def total_kernel(part_ref, out_ref, held, sub, wide, send_1, recv_1, send_2, recv_2):
    row, col = mesh_place()
    barrier = pltpu.get_barrier_semaphore()
    row_partners = [(row, lax.rem(col + s, N_COL)) for s in range(1, N_COL)]
    col_partners = [(lax.rem(row + s, N_ROW), col) for s in range(1, N_ROW)]
    for device in row_partners + col_partners:
        pl.semaphore_signal(barrier, inc=1, device_id=device, device_id_type=MESH)
    pl.semaphore_wait(barrier, N_COL + N_ROW - 2)

    def copies(src, dst, devices, send, recv):
        return [
            pltpu.make_async_remote_copy(
                src_ref=src,
                dst_ref=dst.at[at],
                send_sem=send.at[at],
                recv_sem=recv.at[at],
                device_id=device,
                device_id_type=MESH,
            )
            for at, device in enumerate(devices)
        ]

    first = copies(part_ref, held, row_partners, send_1, recv_1)
    for copy in first:
        copy.start()
    total = part_ref[...]
    for at, copy in enumerate(first):
        copy.wait_recv()
        total += held[at]
    sub[...] = total
    second = copies(sub, wide, col_partners, send_2, recv_2)
    for copy in second:
        copy.start()
    for at, copy in enumerate(second):
        copy.wait_recv()
        total += wide[at]
    out_ref[...] = total
    for copy in first + second:
        copy.wait_send()


def total_everywhere(part):
    vmem = pl.BlockSpec(memory_space=pltpu.VMEM)
    return pl.pallas_call(
        total_kernel,
        out_shape=jax.ShapeDtypeStruct((CA, CP), F32),
        in_specs=[vmem],
        out_specs=vmem,
        scratch_shapes=[
            pltpu.VMEM((N_COL - 1, CA, CP), F32),
            pltpu.VMEM((CA, CP), F32),
            pltpu.VMEM((N_ROW - 1, CA, CP), F32),
            pltpu.SemaphoreType.DMA((N_COL - 1,)),
            pltpu.SemaphoreType.DMA((N_COL - 1,)),
            pltpu.SemaphoreType.DMA((N_ROW - 1,)),
            pltpu.SemaphoreType.DMA((N_ROW - 1,)),
        ],
        compiler_params=pltpu.CompilerParams(
            collective_id=2, has_side_effects=True, vmem_limit_bytes=VMEM_LIMIT
        ),
        name="total_everywhere",
    )(part)


def shards(
    pair_repr,
    pair_gain,
    proj_weight,
    query_weight,
    key_weight,
    mlp_first,
    mlp_second,
    mlp_third,
    atom_feats,
    token_counts,
    key_start,
    pair_cotangent,
):
    gain = pair_gain.reshape(1, CP)
    zrow, corner = project_band(pair_repr, gain, proj_weight)
    patch, patch_corner, *halo = scatter_band(zrow, corner, atom_feats, token_counts)
    key_sums, query_sums, token_sums, blank = atom_pairs(
        key_start,
        pair_cotangent,
        atom_feats,
        halo[:2],
        token_counts,
        halo[2:],
        patch,
        patch_corner,
        (query_weight, key_weight, mlp_first, mlp_second, mlp_third),
    )
    from_before, from_after, patches, corner_sums = gather_gradients(key_sums, token_sums)
    pair_grad, atom_grad, part = finish(
        pair_repr,
        gain,
        proj_weight,
        patches,
        corner_sums,
        blank,
        key_sums,
        (from_before, from_after),
        query_sums,
        atom_feats,
    )
    proj_grad = total_everywhere(part).T
    return pair_grad, atom_grad, proj_grad


def solution(mesh):
    placed = (
        P("row", "col", None),
        P(),
        P(),
        P(),
        P(),
        P(),
        P(),
        P(),
        P(("row", "col"), None),
        P("row", None),
        P(("row", "col")),
        P(("row", "col"), None),
    )
    return jax.shard_map(
        shards,
        mesh=mesh,
        in_specs=placed,
        out_specs=(P("row", "col", None), P(("row", "col"), None), P()),
        check_vma=False,
    )
```

time: 343 us -> 96.7 us (0.28); the launches traced: 337 us -> 96 us
  Pallas kernels: 0 us -> 89.8 us
  matrix products: 73.4 us -> 0 us
  waiting for transfers between devices: 69.6 us -> 0 us
  blocking collectives: 64.9 us -> 0 us
  local copies, waits for them, and re-layouts: 56 us -> 5.49 us
  other arithmetic: 32.1 us -> 0 us
  between operations: 25.8 us -> 0.68 us
  starting transfers between devices: 14.8 us -> 0 us
    pallas_call x0 -> x6, Pallas kernels: none -> 89.8 us  [the longest x1 37.8 us: atom_pairs(): pl.pallas_call(pair_kernel, out_shape=(jax.ShapeDtypeStruct((EXT, CP), F3...]
    dot_general x79 -> x0, matrix products: 73.4 us -> none  [the longest x1 22.9 us: shards(): jnp.einsum('ijc,dc->ijd', tile_grad, proj_weight.astype(jnp.float32), pre...]
    reduce_scatter x1 -> x0, waiting for transfers between devices: 66.8 us -> none  [shards(): lax.psum_scatter(row_grad, 'col', scatter_dimension=1, tiled=True)]
    psum x1 -> x0, blocking collectives: 64.9 us -> none  [shards(): proj_grad = lax.psum(weight_part, ('row', 'col'))]
    convert_element_type x4 -> x0, other arithmetic: 20.2 us -> none  [the longest x1 14.3 us: norm_back(): (inv_scale * (scaled - first_mean - hatted * second_mean)).astype(jnp.bfl...]
    slice x31 -> x0, local copies, waits for them, and re-layouts: 20.2 us -> none  [the longest x17 12.6 us: shards(): cotangent = cot_all[lower:lower + QBLK] * valid_part[None, :, None]]
    reshape x3 -> x0, local copies, waits for them, and re-layouts: 14.9 us -> none  [the longest x1 9.84 us: shards(): tile_proj.astype(jnp.bfloat16).reshape(tok_rows, tok_cols * pair_width)]
    ppermute x6 -> x0, starting transfers between devices: 14.7 us -> none  [the longest x2 6.19 us: with_halo(): lax.ppermute(tail, axis, [(i, (i + 1) % count) for i in range(ends)])]
  transfers between devices with their start and end apart: 8 -> 0, of which waited for: 3 -> 0; matrix products, arithmetic and copies ran while one was open for 7% -> 0% of each run, Pallas kernels for 0% -> 0%
where the time goes in v1:
time: 96.7 us; the launch traced here: 96 us
  Pallas kernels  89.8 us (93%)
  local copies, waits for them, and re-layouts  5.49 us (6%)
    pallas_call x1, Pallas kernels, atom_pairs(): pl.pallas_call(pair_kernel, out_shape=(jax.ShapeDtypeStruct((EXT, CP), F3...  37.8 us
    pallas_call x1, Pallas kernels, total_everywhere(): pl.pallas_call(total_kernel, out_shape=jax.ShapeDtypeStruct((CA, CP), F32...  13.1 us
    pallas_call x1, Pallas kernels, scatter_band(): pl.pallas_call(scatter_kernel, out_shape=(jax.ShapeDtypeStruct((KEYS, QTO...  12.1 us
    pallas_call x1, Pallas kernels, finish(): pl.pallas_call(finish_kernel, out_shape=(jax.ShapeDtypeStruct((TOK, COLS,...  10.3 us
    pallas_call x1, Pallas kernels, gather_gradients(): pl.pallas_call(gather_kernel, out_shape=(jax.ShapeDtypeStruct((HALO, CP),...  9.99 us
    pallas_call x1, Pallas kernels, project_band(): pl.pallas_call(project_kernel, out_shape=(jax.ShapeDtypeStruct((128, TOK...  6.61 us
    unnamed x4, local copies, waits for them, and re-layouts  5.49 us

profile of v1, /device:TPU:0, one launch (start us, length us, event | category | flops | bytes accessed | tf_op | source)
XLA Modules:
  0.0 96.0 jit_solution(10686318623112964558)
XLA Ops:
  0.6 1.4 %copy.19.proj_ref = bf16[128,16]{1,0:T(8,128)(2,1)} copy(bf16[128,16]{0,1:T(8,128)(2,1)} %param.14) | data formatting | bytes 8192 | tf_op args[2]
  2.0 1.4 %copy.17.query_w_ref = bf16[128,16]{1,0:T(8,128)(2,1)} copy(bf16[128,16]{0,1:T(8,128)(2,1)} %param.15) | data formatting | bytes 8192 | tf_op args[3]
  3.4 1.4 %copy.18.key_w_ref = bf16[128,16]{1,0:T(8,128)(2,1)} copy(bf16[128,16]{0,1:T(8,128)(2,1)} %param.16) | data formatting | bytes 8192 | tf_op args[4]
  4.8 6.6 %project_band.1 = (bf16[128,1536]{1,0:T(8,128)(2,1)}, bf16[16,256]{1,0:T(8,128)(2,1)}) custom-call(bf16[96,192,128]{2,1,0:T(8,128)(2,1)} %pair_ref.3, f32[1,128]{1,0:T(1,128)} %bitcast.3, bf16[128,16]{1,0:T(8,128)(2,1)} %copy.19.proj_ref), custom_call_target="tpu_custom_call" | custom-call | tf_op jit(solution)/shard_map/project_band/pallas_call | solution.py:176
  11.4 12.1 %scatter_band.1 = (bf16[48,512]{1,0:T(8,128)(2,1)}, bf16[16,256]{1,0:T(8,128)(2,1)}, bf16[96,128]{1,0:T(8,128)(2,1)}, bf16[96,128]{1,0:T(8,128)(2,1)}, s32[1,96]{1,0:T(1,128)}, /*index=5*/s32[1,96]{1,0:T(1,128)}) custom-call(bf16[128,1536]{1,0:T(8,128)(2,1)} %get-tuple-element.22.zrow_ref, bf16[16,256]{1,0:T(8,128)(2,1)} %get-tuple-element.23.corner_ref, ...), custom_call_target="tpu_custom_call" | custom-call | tf_op jit(solution)/shard_map/scatter_band/pallas_call | solution.py:370
  23.5 37.8 %atom_pairs.1 = (f32[448,128]{1,0:T(8,128)}, f32[256,128]{1,0:T(8,128)}, f32[48,512]{1,0:T(8,128)}, bf16[96,192,128]{2,1,0:T(8,128)(2,1)}) custom-call(s32[8]{0:T(128)} %start_ref.1, bf16[256,2048]{1,0:T(8,128)(2,1)} %cot_ref.1, bf16[256,128]{1,0:T(8,128)(2,1)} %feats_ref.5, bf16[96,128]{1,0:T(8,128)(2,1)} %get-tuple-element.24.feats_before_ref, ...), custom_call_target="tpu_custom_call" | custom-call | tf_op jit(solution)/shard_map/atom_pairs/pallas_call | solution.py:655
  61.3 10.0 %gather_gradients.1 = (f32[96,128]{1,0:T(8,128)}, f32[96,128]{1,0:T(8,128)}, f32[8,48,512]{2,1,0:T(8,128)}, f32[16,256]{1,0:T(8,128)}) custom-call(f32[448,128]{1,0:T(8,128)} %get-tuple-element.30.key_ref, f32[48,512]{1,0:T(8,128)} %get-tuple-element.31.token_ref), custom_call_target="tpu_custom_call" | custom-call | tf_op jit(solution)/shard_map/gather_gradients/pallas_call | solution.py:800
  71.3 10.3 %finish.1 = (bf16[96,192,128]{2,1,0:T(8,128)(2,1)}, bf16[256,128]{1,0:T(8,128)(2,1)}, f32[16,128]{1,0:T(8,128)}) custom-call(bf16[96,192,128]{2,1,0:T(8,128)(2,1)} %pair_ref.3, f32[1,128]{1,0:T(1,128)} %bitcast.4, bf16[128,16]{1,0:T(8,128)(2,1)} %copy.19.proj_ref, f32[8,48,512]{2,1,0:T(8,128)} %get-tuple-element.32.patches_ref, ...), custom_call_target="tpu_custom_call", output_to_operand_aliasing={{0}: (5, {})} | custom-call | tf_op jit(solution)/shard_map/finish/pallas_call | solution.py:976
  81.6 13.1 %total_everywhere.1 = f32[16,128]{1,0:T(8,128)} custom-call(f32[16,128]{1,0:T(8,128)} %get-tuple-element.40.part_ref), custom_call_target="tpu_custom_call" | custom-call | tf_op jit(solution)/shard_map/total_everywhere/pallas_call | solution.py:1044
  94.7 1.3 %copy.22 = f32[128,16]{0,1:T(8,128)} copy(f32[128,16]{0,1:T(8,128)} %bitcast.2) | data formatting | bytes 16384

commit v2 on v0

v2 whole, which is shorter than its diff:
```python
import jax
import jax.numpy as jnp
from jax import lax
from jax.experimental import pallas as pl
from jax.experimental.pallas import tpu as pltpu
from jax.sharding import PartitionSpec as P

F32 = jnp.float32
BF16 = jnp.bfloat16
MESH = pl.DeviceIdType.MESH

N_ROW = 16
N_COL = 8
TOK = 96
COLS = 192
CP = 128
CA = 16
QBLK = 32
KWIN = 128
MOST = 23
ATOMS = 256
ROW_ATOMS = 2048
SLACK = TOK * MOST - ROW_ATOMS
HALO = KWIN - QBLK
EXT = ATOMS + 2 * HALO
NBLK = ATOMS // QBLK
LANES = QBLK * CA
KEYS = 48
QTOK = 32
GROUPS = TOK // 8
VMEM_LIMIT = 56 * 1024 * 1024


def key_base(col):
    return 16 * ((11 * col - 5 + 16) // 16) - 16


def query_base(col):
    return jnp.minimum(8 * ((11 * col) // 8), TOK - QTOK)


def query_base_static(col):
    return min(8 * ((11 * col) // 8), TOK - QTOK)


def iota(shape, dim):
    return lax.broadcasted_iota(jnp.int32, shape, dim)


def dot(a, b):
    return jnp.dot(a, b, preferred_element_type=F32)


def dot_nt(a, b):
    return lax.dot_general(a, b, (((1,), (1,)), ((), ())), preferred_element_type=F32)


def dot_tn(a, b):
    return lax.dot_general(a, b, (((0,), (0,)), ((), ())), preferred_element_type=F32)


def split(x):
    high = x.astype(BF16)
    low = (x - high.astype(F32)).astype(BF16)
    return high, low


def dot_split(x, w):
    high, low = split(x)
    return dot(high, w) + dot(low, w)


def sigmoid(x):
    return 0.5 * jnp.tanh(0.5 * x) + 0.5


def mesh_place():
    row = lax.axis_index("row")
    col = lax.axis_index("col")
    return row, col


def normalise(block):
    floats = block.astype(F32)
    centre = floats - jnp.mean(floats, axis=-1, keepdims=True)
    spread = jnp.mean(centre * centre, axis=-1, keepdims=True)
    inv_scale = lax.rsqrt(spread + 1e-05)
    return centre * inv_scale, inv_scale


def channel_eye(rows):
    return ((iota((rows, CA), 0) & (CA - 1)) == iota((rows, CA), 1)).astype(F32).astype(BF16)


def channel_eye_t(lanes):
    return ((iota((CA, lanes), 1) & (CA - 1)) == iota((CA, lanes), 0)).astype(F32).astype(BF16)


def spread_projection(proj):
    eye_t = channel_eye_t(CP)
    wide = dot_tn(proj, eye_t)
    lane = iota((CP, CP), 1) // CA
    return jnp.concatenate(
        [jnp.where(lane == i, wide, 0.0).astype(BF16) for i in range(8)], axis=0
    )


def spread_projection_t(proj):
    eye = channel_eye(CP)
    tall = dot(eye, proj)
    row = iota((CP, CP), 0) // CA
    return jnp.concatenate(
        [jnp.where(row == i, tall, 0.0).astype(BF16) for i in range(8)], axis=1
    )


def window_column(group, odd):
    first = 16 * ((8 * group - 13 + 16) // 16) - 16
    return jnp.clip(first + TOK * odd, 0, COLS - KEYS)


def corner_place(odd):
    return 80 * odd, 176 * (1 - odd)


def swap_groups(pieces, group):
    for bit in (1, 2, 4):
        take = (group & bit) != 0
        swapped = list(pieces)
        for at in range(8):
            if at & bit == 0:
                one, two = pieces[at], pieces[at | bit]
                swapped[at] = jnp.where(take, pltpu.roll(two, CA * bit, 1), one)
                swapped[at | bit] = jnp.where(take, two, pltpu.roll(one, 128 - CA * bit, 1))
        pieces = swapped
    return pieces


def neighbours(row, col):
    ahead = (
        jnp.where(col == N_COL - 1, lax.rem(row + 1, N_ROW), row),
        lax.rem(col + 1, N_COL),
    )
    behind = (
        jnp.where(col == 0, lax.rem(row + N_ROW - 1, N_ROW), row),
        lax.rem(col + N_COL - 1, N_COL),
    )
    return ahead, behind


def tile_owners(row):
    along_z = [4 * (row // 4) + lax.rem(row + step, 4) for step in range(1, 4)]
    along_x = [lax.rem(row + 4 * step, N_ROW) for step in range(1, 4)]
    return [(other, other // 2) for other in along_z], [(other, other // 2) for other in along_x]


def band_kernel(
    start_ref,
    pair_ref,
    cot_hbm,
    gain_ref,
    proj_ref,
    feats_ref,
    counts_ref,
    query_w_ref,
    key_w_ref,
    first_w_ref,
    second_w_ref,
    third_w_ref,
    grads_ref,
    corner_grads_ref,
    atom_grad_ref,
    proj_grad_ref,
    band,
    corner_band,
    flat,
    corner_flat,
    zrow,
    zcorner,
    patch,
    patch_corner,
    feats_before,
    feats_after,
    counts_before,
    counts_after,
    cot_ref,
    act_ext,
    lhs,
    rhs,
    query_high,
    query_low,
    spread,
    cot,
    state,
    mixers,
    key_tiled,
    query_tiled,
    slot_from,
    slot_to,
    hot_ref,
    key_sum,
    query_sum,
    token_sum,
    key_before,
    key_after,
    patches,
    token_corner,
    tokens,
    tokens_high,
    tokens_low,
    weight_part,
    weight_corner,
    weight_z,
    weight_x,
    weight_total,
    load_sems,
    cot_sem,
    corner_load_sem,
    send_z,
    recv_z,
    send_c,
    recv_c,
    send_h,
    recv_h,
    send_t,
    recv_t,
    send_tc,
    recv_tc,
    send_k,
    recv_k,
    send_wc,
    recv_wc,
    send_wz,
    recv_wz,
    send_wx,
    recv_wx,
    send_w,
    recv_w,
):
    row = lax.axis_index("row")
    col = lax.axis_index("col")
    odd = row % 2
    half = row // 2
    is_main = col == half
    not_main = col != half
    holder = jnp.where(odd == 0, half - 1, half + 1)
    reader = (N_COL - 1) * odd
    exists = (holder >= 0) & (holder < N_COL)
    is_holder = exists & (col == holder)
    is_reader = exists & (col == reader)
    same_device = holder == reader
    other_device = holder != reader
    holder_col = jnp.clip(holder, 0, N_COL - 1)
    ahead, behind = neighbours(row, col)
    along_z, along_x = tile_owners(row)

    def remote(src, dst, send, recv, device):
        return pltpu.make_async_remote_copy(
            src_ref=src,
            dst_ref=dst,
            send_sem=send,
            recv_sem=recv,
            device_id=device,
            device_id_type=MESH,
        )

    def window_copy(group):
        first = pl.multiple_of(window_column(group, odd), 16)
        return pltpu.make_async_copy(
            pair_ref.at[pl.ds(8 * group, 8), pl.ds(first, KEYS)],
            band.at[group],
            load_sems.at[group],
        )

    first_row, first_col = corner_place(odd)
    corner_load = pltpu.make_async_copy(
        pair_ref.at[pl.ds(first_row, 16), pl.ds(pl.multiple_of(first_col, 16), 16)],
        corner_band,
        corner_load_sem,
    )
    cot_load = pltpu.make_async_copy(cot_hbm, cot_ref, cot_sem)

    @pl.when(is_main)
    def _():
        for group in range(GROUPS):
            window_copy(group).start()

    @pl.when(is_holder)
    def _():
        corner_load.start()

    cot_load.start()

    barrier = pltpu.get_barrier_semaphore()

    def greet(device):
        pl.semaphore_signal(barrier, inc=1, device_id=device, device_id_type=MESH)

    greet(ahead)
    greet(behind)

    @pl.when(not_main)
    def _():
        greet((row, half))

    @pl.when(is_main)
    def _():
        for step in range(1, N_COL):
            greet((row, lax.rem(col + step, N_COL)))
        for device in along_z + along_x:
            greet(device)

    @pl.when(is_holder & other_device)
    def _():
        greet((row, reader))

    @pl.when(is_reader & other_device)
    def _():
        greet((row, holder_col))

    greeted = 2 + jnp.where(is_main, N_COL - 1 + 6, 1)
    greeted += jnp.where((is_holder | is_reader) & other_device, 1, 0)

    @pl.when(is_main)
    def _():
        zrow[...] = jnp.zeros_like(zrow)
        spread_w = spread_projection(proj_ref[...])
        gain = gain_ref[...]

        def project(group, carry):
            window_copy(group).wait()
            hatted, _ = normalise(band[group])
            normed = (hatted * gain).astype(BF16)
            rows = jnp.concatenate([normed[i] for i in range(8)], axis=1)
            flat[pl.ds(pl.multiple_of(KEYS * group, 16), KEYS), :] = rows
            at = pl.multiple_of(window_column(group, odd) - TOK * odd + 16, 16)
            lanes = pl.ds(pl.multiple_of(128 * group, 128), 128)
            zrow[pl.ds(at, KEYS), lanes] = dot(rows, spread_w).astype(BF16)
            return carry

        lax.fori_loop(0, GROUPS, project, 0)

    @pl.when(is_holder)
    def _():
        spread_w = spread_projection(proj_ref[...])
        corner_load.wait()
        hatted, _ = normalise(corner_band[...])
        normed = (hatted * gain_ref[...]).astype(BF16)
        for part in range(2):
            rows = jnp.concatenate([normed[8 * part + i] for i in range(8)], axis=1)
            corner_flat[16 * part : 16 * part + 16, :] = rows
            zcorner[:, 128 * part : 128 * part + 128] = dot(rows, spread_w).astype(BF16)

    pl.semaphore_wait(barrier, greeted)

    def z_part(target, first):
        return zrow.at[pl.ds(key_base(target) + 16, KEYS), pl.ds(first, QTOK * CA)]

    def z_copy(target):
        src = z_part(target, query_base_static(target) * CA)
        return remote(src, patch, send_z.at[target], recv_z, (row, target))

    corner_copy = remote(zcorner, patch_corner, send_c, recv_c, (row, reader))

    @pl.when(is_main)
    def _():
        for target in range(N_COL):

            @pl.when(col != target)
            def _():
                z_copy(target).start()

        patch[...] = zrow[
            pl.ds(pl.multiple_of(key_base(col) + 16, 16), KEYS),
            pl.ds(pl.multiple_of(query_base(col) * CA, 128), QTOK * CA),
        ]

    @pl.when(is_holder & other_device)
    def _():
        corner_copy.start()

    @pl.when(is_holder & same_device)
    def _():
        patch_corner[...] = zcorner[...]

    halos = [
        remote(src, dst, send_h.at[at], recv_h.at[at], device)
        for at, (src, dst, device) in enumerate(
            (
                (feats_ref.at[pl.ds(ATOMS - HALO, HALO)], feats_before, ahead),
                (feats_ref.at[pl.ds(0, HALO)], feats_after, behind),
                (counts_ref, counts_before, ahead),
                (counts_ref, counts_after, behind),
            )
        )
    ]
    for copy in halos:
        copy.start()

    eye = channel_eye(LANES)
    eye16 = eye[:256]
    same = (iota((256, 256), 0) // CA) == (iota((256, 256), 1) // CA)

    def mixer(weight, flip):
        left = dot_nt(eye16, weight) if flip else dot(eye16, weight)
        wide = dot_nt(left.astype(BF16), eye16)
        return jnp.where(same, wide, 0.0).astype(BF16)

    mixers[0] = mixer(first_w_ref[...], False)
    mixers[1] = mixer(second_w_ref[...], False)
    mixers[2] = mixer(third_w_ref[...], True)
    mixers[3] = mixer(second_w_ref[...], True)
    mixers[4] = mixer(first_w_ref[...], True)
    key_tiled[...] = dot(eye, key_w_ref[...]).astype(BF16)
    query_tiled[...] = dot(eye, query_w_ref[...]).astype(BF16)
    eye_t = channel_eye_t(LANES)
    rhs[128:256, :] = dot_tn(key_w_ref[...], eye_t).astype(BF16)
    rhs[112:128, :] = jnp.zeros((16, LANES), BF16)

    def activate(feats):
        floats = feats.astype(F32)
        return floats * jax.nn.sigmoid(floats)

    own_act = activate(feats_ref[...]).astype(BF16)
    act_ext[HALO : HALO + ATOMS] = activate(feats_ref[...])

    lane_is_row = iota((QBLK, LANES), 1) // CA == iota((QBLK, LANES), 0)
    query_wide = dot_tn(query_w_ref[...], eye_t).astype(BF16)
    for block in range(NBLK):
        terms = dot(own_act[QBLK * block : QBLK * block + QBLK], query_wide)
        high, low = split(jnp.where(lane_is_row, terms, 0.0))
        query_high[QBLK * block : QBLK * block + QBLK] = high
        query_low[QBLK * block : QBLK * block + QBLK] = low

    own = counts_ref[...].astype(F32)

    def rows_of(counts, rows):
        return jnp.broadcast_to(counts, (rows, TOK)).astype(BF16)

    def as_mask(flag):
        return jnp.where(flag, 1.0, 0.0).astype(BF16)

    first_query = query_base(col)
    slot = iota((LANES, TOK), 0) // CA + first_query
    slot_index = iota((LANES, TOK), 1)
    own_rows = rows_of(own, 128)
    slot_from[...] = dot_nt(as_mask(slot_index < slot), own_rows)
    slot_to[...] = dot_nt(as_mask(slot_index < slot + 1), own_rows)

    lane_atom_row = (iota((1, LANES), 1) // CA).astype(F32)
    channel_match = (iota((256, 128), 0) % CA) == (iota((256, 128), 1) % CA)

    def block_place(block):
        first = col * ATOMS + block * QBLK
        token = 8 * (first // (8 * MOST)) - first_query
        return first, pl.multiple_of(token * CA, 128)

    def query_hot(block):
        first, at = block_place(block)
        low = slot_from[pl.ds(at, 256), :]
        high = slot_to[pl.ds(at, 256), :]
        parts = []
        for part in range(4):
            atom = lane_atom_row[:, 128 * part : 128 * part + 128] + first.astype(F32)
            hot = (low <= atom) & (atom < high) & channel_match
            parts.append(jnp.where(hot, 1.0, 0.0).astype(BF16))
        return jnp.concatenate(parts, axis=1)

    def key_first(block):
        return col * ATOMS + block * QBLK + start_ref[block]

    def hot_step(block, carry):
        hot_ref[block] = query_hot(block)
        return carry

    lax.fori_loop(0, NBLK, hot_step, 0)

    cot_load.wait()

    group = iota((16, 128), 1) // CA

    def spread_step(eight, carry):
        rows = cot_ref[pl.ds(pl.multiple_of(16 * eight, 16), 16), :].astype(F32)
        for half in range(2):
            at = pl.multiple_of(256 * eight + 128 * half, 128)
            for chunk in range(16):
                spread[pl.ds(at + 8 * chunk, 8), :] = rows[
                    8 * half : 8 * half + 8, 128 * chunk : 128 * chunk + 128
                ]
        return carry

    lax.fori_loop(0, ATOMS // 16, spread_step, 0)

    def swap_step(eight, carry):
        at = 128 * eight
        pieces = [spread[pl.ds(at + atom, 16, stride=8), :] for atom in range(8)]
        pieces = swap_groups(pieces, group)
        to = NBLK * KWIN * (eight % 4) + KWIN * (eight // 4)
        for key in range(8):
            cot[pl.ds(to + key, 16, stride=8), :] = pieces[key]
        return carry

    lax.fori_loop(0, ATOMS // 8, swap_step, 0)

    for copy in halos:
        copy.wait()
    act_ext[0:HALO] = activate(feats_before[...])
    act_ext[HALO + ATOMS : EXT] = activate(feats_after[...])

    base = key_base(col)
    before = counts_before[...].astype(F32)
    after = counts_after[...].astype(F32)

    def lane_bounds(offset):
        token = iota((TOK, 128), 1) + (base + offset)
        index = iota((TOK, 128), 0)
        total = dot(rows_of(own, 8), as_mask(index < token))
        total += dot(rows_of(after, 8), as_mask(index + TOK < token))
        return total - dot(rows_of(before, 8), as_mask(index - TOK >= token))

    def column_bounds(offset):
        token = iota((KEYS, TOK), 0) + (base + offset)
        index = iota((KEYS, TOK), 1)
        total = dot_nt(as_mask(index < token), rows_of(own, 128))
        total += dot_nt(as_mask(index + TOK < token), rows_of(after, 128))
        return total - dot_nt(as_mask(index - TOK >= token), rows_of(before, 128))

    lane = iota((8, 128), 1)
    far = 1.0e6
    lane_from = jnp.where(lane < 48, lane_bounds(0), jnp.where(lane < 112, -far, far))[0:1]
    lane_to = jnp.where(lane < 48, lane_bounds(1), jnp.where(lane < 112, far, -far))[0:1]
    column_from = column_bounds(0)
    column_to = column_bounds(1)

    @pl.when(is_main)
    def _():
        for target in range(N_COL):

            @pl.when(col != target)
            def _():
                z_copy(target).wait_send()

    @pl.when(not_main)
    def _():
        z_copy(0).wait_recv()

    @pl.when(is_holder & other_device)
    def _():
        corner_copy.wait_send()

    @pl.when(is_reader & other_device)
    def _():
        corner_copy.wait_recv()

    @pl.when(is_reader)
    def _():
        at = pl.multiple_of(32 * odd, 16), pl.multiple_of(256 * odd, 128)
        patch[pl.ds(at[0], 16), pl.ds(at[1], 256)] = patch_corner[...]

    def start_step(block, carry):
        _, at = block_place(block)
        hot = hot_ref[block]
        window = start_ref[block] + block * QBLK + HALO
        atom = (iota((KWIN, 128), 0) + key_first(block)).astype(F32)
        lhs[:, 0:128] = as_mask((lane_from <= atom) & (atom < lane_to))
        lhs[:, 128:256] = act_ext[pl.ds(window, KWIN), :].astype(BF16)
        rhs[0:48, :] = dot(patch[:, pl.ds(at, 256)], hot).astype(BF16)
        mine = pl.multiple_of(block * QBLK, QBLK)
        rhs[48:80, :] = query_high[pl.ds(mine, QBLK), :]
        rhs[80:112, :] = query_low[pl.ds(mine, QBLK), :]
        state[pl.ds(pl.multiple_of(block * KWIN, KWIN), KWIN), :] = dot(lhs[...], rhs[...])
        return carry

    lax.fori_loop(0, NBLK, start_step, 0)

    atom_low = jnp.where(row == 0, 0, -ROW_ATOMS)
    atom_high = jnp.where(row == N_ROW - 1, ROW_ATOMS, 2 * ROW_ATOMS)

    def slope(value, sigma, act):
        return sigma + act - act * sigma

    def mlp_step(step, carry):
        pair = step // 2
        at = pl.multiple_of(256 * pair, 256)
        place = pl.ds(at, 256), pl.ds(pl.multiple_of(256 * (step % 2), 256), 256)
        value = state[place]
        index = iota((256, 256), 0)
        begin = jnp.where(index < KWIN, key_first(2 * pair), key_first(2 * pair + 1) - KWIN)
        atom = index + begin
        parts = [
            cot[pl.ds(pl.multiple_of(at + NBLK * KWIN * (2 * (step % 2) + part), 256), 256), :]
            for part in range(2)
        ]
        grad = jnp.concatenate(parts, axis=1)
        grad = jnp.where((atom >= atom_low) & (atom < atom_high), grad, 0.0)
        sig_0 = sigmoid(value)
        act_0 = value * sig_0
        one = dot_split(act_0, mixers[0])
        sig_1 = sigmoid(one)
        act_1 = one * sig_1
        two = dot_split(act_1, mixers[1])
        sig_2 = sigmoid(two)
        back = dot(grad.astype(BF16), mixers[2]) * slope(two, sig_2, two * sig_2)
        back = dot_split(back, mixers[3]) * slope(one, sig_1, act_1)
        back = dot_split(back, mixers[4]) * slope(value, sig_0, act_0)
        state[place] = grad + back
        return carry

    lax.fori_loop(0, 8, mlp_step, 0)

    key_sum[...] = jnp.zeros_like(key_sum)
    token_sum[...] = jnp.zeros_like(token_sum)

    def sum_step(block, carry):
        _, at = block_place(block)
        window = start_ref[block] + block * QBLK + HALO
        back = state[pl.ds(pl.multiple_of(block * KWIN, KWIN), KWIN), :]
        high, low = split(back)
        by_key = dot(high, key_tiled[...]) + dot(low, key_tiled[...])
        reach = KWIN + HALO
        moved = as_mask(
            iota((reach, KWIN), 0) == iota((reach, KWIN), 1) + (start_ref[block] + HALO)
        )
        by_key_high, by_key_low = split(by_key)
        key_sum[pl.ds(pl.multiple_of(block * QBLK, QBLK), reach), :] += dot(
            moved, by_key_high
        ) + dot(moved, by_key_low)
        over_keys = jnp.sum(back, axis=0, keepdims=True)
        over_keys = jnp.where(lane_is_row, over_keys, 0.0)
        mine = pl.multiple_of(block * QBLK, QBLK)
        query_sum[pl.ds(mine, QBLK), :] = dot_split(over_keys, query_tiled[...])
        atom = (iota((KEYS, 128), 1) + key_first(block)).astype(F32)
        key_hot = as_mask((column_from <= atom) & (atom < column_to))
        by_token = dot(key_hot, high) + dot(key_hot, low)
        high, low = split(by_token)
        hot = hot_ref[block]
        token_sum[:, pl.ds(at, 256)] += dot_nt(high, hot) + dot_nt(low, hot)
        return carry

    lax.fori_loop(0, NBLK, sum_step, 0)

    def token_copy(source):
        return remote(token_sum, patches.at[source], send_t, recv_t.at[source], (row, half))

    corner_part = token_sum.at[
        pl.ds(pl.multiple_of(32 * odd, 16), 16), pl.ds(pl.multiple_of(256 * odd, 128), 256)
    ]
    token_corner_copy = remote(corner_part, token_corner, send_tc, recv_tc, (row, holder_col))

    @pl.when(not_main)
    def _():
        token_copy(col).start()

    @pl.when(is_main)
    def _():
        patches[col] = token_sum[...]

    @pl.when(is_reader & other_device)
    def _():
        token_corner_copy.start()

    @pl.when(is_reader & same_device)
    def _():
        token_corner[...] = corner_part[...]

    key_halos = [
        remote(src, dst, send_k.at[at], recv_k.at[at], device)
        for at, (src, dst, device) in enumerate(
            (
                (key_sum.at[pl.ds(HALO + ATOMS, HALO)], key_before, ahead),
                (key_sum.at[pl.ds(0, HALO)], key_after, behind),
            )
        )
    ]
    for copy in key_halos:
        copy.start()

    def diagonal(wide):
        total = wide[0:CA, 0:128]
        for i in range(1, 8):
            total += wide[CA * i : CA * i + CA, 128 * i : 128 * i + 128]
        return total

    def gradient(block, rows_high, rows_low, spread_w, gain):
        hatted, inv_scale = normalise(block)
        wide = dot(rows_high, spread_w) + dot(rows_low, spread_w)
        scaled = jnp.stack([wide[:, 128 * i : 128 * i + 128] for i in range(8)]) * gain
        first_mean = jnp.mean(scaled, axis=-1, keepdims=True)
        second_mean = jnp.mean(scaled * hatted, axis=-1, keepdims=True)
        return (inv_scale * (scaled - first_mean - hatted * second_mean)).astype(BF16)

    corner_weight_copy = remote(
        weight_part, weight_corner, send_wc, recv_wc, (row, half)
    )

    @pl.when(is_holder)
    def _():
        @pl.when(other_device)
        def _():
            token_corner_copy.wait_recv()

        spread_w = spread_projection_t(proj_ref[...])
        gain = gain_ref[...]
        total = jnp.zeros((CA, CP), F32)
        for part in range(2):
            high, low = split(token_corner[:, 128 * part : 128 * part + 128])
            rows = corner_flat[16 * part : 16 * part + 16, :]
            total += diagonal(dot_tn(high, rows) + dot_tn(low, rows))
        weight_part[...] = total
        corner_weight_copy.start()
        for part in range(2):
            high, low = split(token_corner[:, 128 * part : 128 * part + 128])
            corner_grads_ref[part] = gradient(
                corner_band[8 * part : 8 * part + 8], high, low, spread_w, gain
            )

    z_copies = [
        remote(weight_part, weight_z.at[at], send_wz.at[at], recv_wz.at[at], device)
        for at, device in enumerate(along_z)
    ]
    x_copies = [
        remote(weight_total.at[0], weight_x.at[at], send_wx.at[at], recv_wx.at[at], device)
        for at, device in enumerate(along_x)
    ]

    def total_copy(target):
        return remote(
            weight_total.at[1], weight_total.at[1], send_w.at[target], recv_w, (row, target)
        )

    @pl.when(is_main)
    def _():
        tokens[...] = jnp.zeros_like(tokens)
        for source in range(N_COL):

            @pl.when(col != source)
            def _():
                token_copy(source).wait_recv()

            at = key_base(source) + 16
            lanes = query_base_static(source) * CA
            tokens[at : at + KEYS, lanes : lanes + QTOK * CA] += patches[source]

        def cut(group, carry):
            at = pl.multiple_of(window_column(group, odd) - TOK * odd + 16, 16)
            lanes = pl.ds(pl.multiple_of(128 * group, 128), 128)
            high, low = split(tokens[pl.ds(at, KEYS), lanes])
            to = pl.ds(pl.multiple_of(KEYS * group, 16), KEYS)
            tokens_high[to, :] = high
            tokens_low[to, :] = low
            return carry

        lax.fori_loop(0, GROUPS, cut, 0)
        total = diagonal(
            dot_tn(tokens_high[...], flat[...]) + dot_tn(tokens_low[...], flat[...])
        )

        @pl.when(exists)
        def _():
            corner_weight_copy.wait_recv()

        total += jnp.where(exists, weight_corner[...], 0.0)
        weight_part[...] = total
        for copy in z_copies:
            copy.start()
        spread_w = spread_projection_t(proj_ref[...])
        gain = gain_ref[...]

        def grad_step(group, carry):
            rows = pl.ds(pl.multiple_of(KEYS * group, 16), KEYS)
            grads_ref[group] = gradient(
                band[group], tokens_high[rows, :], tokens_low[rows, :], spread_w, gain
            )
            return carry

        lax.fori_loop(0, GROUPS // 2, grad_step, 0)
        for at, copy in enumerate(z_copies):
            copy.wait_recv()
            total += weight_z[at]
        weight_total[0] = total
        for copy in x_copies:
            copy.start()
        lax.fori_loop(GROUPS // 2, GROUPS, grad_step, 0)
        for at, copy in enumerate(x_copies):
            copy.wait_recv()
            total += weight_x[at]
        weight_total[1] = total
        for target in range(N_COL):

            @pl.when(col != target)
            def _():
                total_copy(target).start()

    for copy in key_halos:
        copy.wait()
    total = query_sum[...] + key_sum[HALO : HALO + ATOMS]
    lead = total[:HALO] + key_before[...]
    trail = total[ATOMS - HALO :] + key_after[...]
    total = jnp.concatenate([lead, total[HALO : ATOMS - HALO], trail], axis=0)
    floats = feats_ref[...].astype(F32)
    sigma = jax.nn.sigmoid(floats)
    atom_grad_ref[...] = (total * (sigma * (1.0 + floats * (1.0 - sigma)))).astype(BF16)

    @pl.when(not_main)
    def _():
        token_copy(col).wait_send()

    @pl.when(is_reader & other_device)
    def _():
        token_corner_copy.wait_send()

    @pl.when(is_holder)
    def _():
        corner_weight_copy.wait_send()

    @pl.when(is_main)
    def _():
        for copy in z_copies + x_copies:
            copy.wait_send()
        for target in range(N_COL):

            @pl.when(col != target)
            def _():
                total_copy(target).wait_send()

    @pl.when(not_main)
    def _():
        total_copy(0).wait_recv()

    proj_grad_ref[...] = weight_total[1]


def band_pass(start, pair_repr, cot, gain, proj, feats, counts, weights):
    vmem = pl.BlockSpec(memory_space=pltpu.VMEM)
    any_spec = pl.BlockSpec(memory_space=pl.ANY)
    dma = pltpu.SemaphoreType.DMA
    return pl.pallas_call(
        band_kernel,
        out_shape=(
            jax.ShapeDtypeStruct((GROUPS, 8, KEYS, CP), BF16),
            jax.ShapeDtypeStruct((2, 8, 16, CP), BF16),
            jax.ShapeDtypeStruct((ATOMS, CP), BF16),
            jax.ShapeDtypeStruct((CA, CP), F32),
        ),
        in_specs=[pl.BlockSpec(memory_space=pltpu.SMEM), any_spec, any_spec] + [vmem] * 9,
        out_specs=(vmem,) * 4,
        scratch_shapes=[
            pltpu.VMEM((GROUPS, 8, KEYS, CP), BF16),
            pltpu.VMEM((16, 16, CP), BF16),
            pltpu.VMEM((GROUPS * KEYS, 8 * CP), BF16),
            pltpu.VMEM((32, 8 * CP), BF16),
            pltpu.VMEM((128, TOK * CA), BF16),
            pltpu.VMEM((16, 256), BF16),
            pltpu.VMEM((KEYS, QTOK * CA), BF16),
            pltpu.VMEM((16, 256), BF16),
            pltpu.VMEM((HALO, CP), BF16),
            pltpu.VMEM((HALO, CP), BF16),
            pltpu.VMEM((1, TOK), jnp.int32),
            pltpu.VMEM((1, TOK), jnp.int32),
            pltpu.VMEM((ATOMS, KWIN * CA), BF16),
            pltpu.VMEM((EXT, CP), F32),
            pltpu.VMEM((KWIN, 256), BF16),
            pltpu.VMEM((256, LANES), BF16),
            pltpu.VMEM((ATOMS, LANES), BF16),
            pltpu.VMEM((ATOMS, LANES), BF16),
            pltpu.VMEM((ATOMS * 16, 128), F32),
            pltpu.VMEM((4 * NBLK * KWIN, 128), F32),
            pltpu.VMEM((NBLK * KWIN, LANES), F32),
            pltpu.VMEM((5, 256, 256), BF16),
            pltpu.VMEM((LANES, CP), BF16),
            pltpu.VMEM((LANES, CP), BF16),
            pltpu.VMEM((LANES, 128), F32),
            pltpu.VMEM((LANES, 128), F32),
            pltpu.VMEM((NBLK, 256, LANES), BF16),
            pltpu.VMEM((EXT, CP), F32),
            pltpu.VMEM((ATOMS, CP), F32),
            pltpu.VMEM((KEYS, QTOK * CA), F32),
            pltpu.VMEM((HALO, CP), F32),
            pltpu.VMEM((HALO, CP), F32),
            pltpu.VMEM((N_COL, KEYS, QTOK * CA), F32),
            pltpu.VMEM((16, 256), F32),
            pltpu.VMEM((128, TOK * CA), F32),
            pltpu.VMEM((GROUPS * KEYS, 128), BF16),
            pltpu.VMEM((GROUPS * KEYS, 128), BF16),
            pltpu.VMEM((CA, CP), F32),
            pltpu.VMEM((CA, CP), F32),
            pltpu.VMEM((3, CA, CP), F32),
            pltpu.VMEM((3, CA, CP), F32),
            pltpu.VMEM((2, CA, CP), F32),
            dma((GROUPS,)),
            dma,
            dma,
            dma((N_COL,)),
            dma,
            dma,
            dma,
            dma((4,)),
            dma((4,)),
            dma,
            dma((N_COL,)),
            dma,
            dma,
            dma((2,)),
            dma((2,)),
            dma,
            dma,
            dma((3,)),
            dma((3,)),
            dma((3,)),
            dma((3,)),
            dma((N_COL,)),
            dma,
        ],
        compiler_params=pltpu.CompilerParams(
            collective_id=0, has_side_effects=True, vmem_limit_bytes=VMEM_LIMIT
        ),
        name="band_pass",
    )(start, pair_repr, cot, gain, proj, feats, counts, *weights)


def place_kernel(
    grads_ref,
    corner_ref,
    atom_ref,
    proj_ref,
    pair_grad_ref,
    atom_grad_ref,
    proj_grad_ref,
    rows,
    zeros,
    load_sems,
    corner_sem,
    store_sems,
):
    row = lax.axis_index("row")
    col = lax.axis_index("col")
    odd = row % 2
    half = row // 2
    is_main = col == half
    holder = jnp.where(odd == 0, half - 1, half + 1)
    is_holder = col == holder
    plain = (col != half) & (col != holder)

    def load(group):
        first = pl.multiple_of(window_column(group, odd), 16)
        return pltpu.make_async_copy(
            grads_ref.at[group], rows.at[group, :, pl.ds(first, KEYS)], load_sems.at[group]
        )

    def store(group, source):
        return pltpu.make_async_copy(
            source, pair_grad_ref.at[pl.ds(8 * group, 8)], store_sems.at[group]
        )

    @pl.when(is_main)
    def _():
        rows[...] = jnp.zeros_like(rows)
        for group in range(GROUPS):
            load(group).start()
        for group in range(GROUPS):
            load(group).wait()
            store(group, rows.at[group]).start()

    zeros[...] = jnp.zeros_like(zeros)

    @pl.when(is_holder)
    def _():
        first_row, first_col = corner_place(odd)
        rows[0:2] = jnp.zeros((2, 8, COLS, CP), BF16)
        copy = pltpu.make_async_copy(
            corner_ref,
            rows.at[pl.ds(0, 2), :, pl.ds(pl.multiple_of(first_col, 16), 16)],
            corner_sem,
        )
        copy.start()
        for group in range(2, GROUPS - 2):
            store(group, zeros).start()
        copy.wait()
        for part in range(2):

            @pl.when(odd == 0)
            def _():
                store(part, rows.at[part]).start()
                store(GROUPS - 2 + part, zeros).start()

            @pl.when(odd == 1)
            def _():
                store(part, zeros).start()
                store(GROUPS - 2 + part, rows.at[part]).start()

    @pl.when(plain)
    def _():
        for group in range(GROUPS):
            store(group, zeros).start()

    atom_grad_ref[...] = atom_ref[...]
    proj_grad_ref[...] = proj_ref[...]
    for group in range(GROUPS):
        store(group, zeros).wait()


def place(grads, corner, atom_grad, proj_grad):
    vmem = pl.BlockSpec(memory_space=pltpu.VMEM)
    any_spec = pl.BlockSpec(memory_space=pl.ANY)
    return pl.pallas_call(
        place_kernel,
        out_shape=(
            jax.ShapeDtypeStruct((TOK, COLS, CP), BF16),
            jax.ShapeDtypeStruct((ATOMS, CP), BF16),
            jax.ShapeDtypeStruct((CA, CP), F32),
        ),
        in_specs=[any_spec, any_spec, vmem, vmem],
        out_specs=(any_spec, vmem, vmem),
        scratch_shapes=[
            pltpu.VMEM((GROUPS, 8, COLS, CP), BF16),
            pltpu.VMEM((8, COLS, CP), BF16),
            pltpu.SemaphoreType.DMA((GROUPS,)),
            pltpu.SemaphoreType.DMA,
            pltpu.SemaphoreType.DMA((GROUPS,)),
        ],
        compiler_params=pltpu.CompilerParams(vmem_limit_bytes=VMEM_LIMIT),
        name="place",
    )(grads, corner, atom_grad, proj_grad)


def shards(
    pair_repr,
    pair_gain,
    proj_weight,
    query_weight,
    key_weight,
    mlp_first,
    mlp_second,
    mlp_third,
    atom_feats,
    token_counts,
    key_start,
    pair_cotangent,
):
    grads, corner, atom_grad, proj_grad = band_pass(
        key_start,
        pair_repr,
        pair_cotangent,
        pair_gain.reshape(1, CP),
        proj_weight.T,
        atom_feats,
        token_counts,
        (query_weight.T, key_weight.T, mlp_first, mlp_second, mlp_third),
    )
    pair_grad, atom_grad, proj_grad = place(grads, corner, atom_grad, proj_grad)
    return pair_grad, atom_grad, proj_grad.T


def solution(mesh):
    placed = (
        P("row", "col", None),
        P(),
        P(),
        P(),
        P(),
        P(),
        P(),
        P(),
        P(("row", "col"), None),
        P("row", None),
        P(("row", "col")),
        P(("row", "col"), None),
    )
    return jax.shard_map(
        shards,
        mesh=mesh,
        in_specs=placed,
        out_specs=(P("row", "col", None), P(("row", "col"), None), P()),
        check_vma=False,
    )
```

time: 343 us -> 57.5 us (0.17); the launches traced: 337 us -> 57.2 us
  matrix products: 73.4 us -> 0 us
  waiting for transfers between devices: 69.6 us -> 0 us
  blocking collectives: 64.9 us -> 0 us
  Pallas kernels: 0 us -> 56.5 us
  local copies, waits for them, and re-layouts: 56 us -> 0 us
  other arithmetic: 32.1 us -> 0 us
  between operations: 25.8 us -> 0.64 us
  starting transfers between devices: 14.8 us -> 0 us
    dot_general x79 -> x0, matrix products: 73.4 us -> none  [the longest x1 22.9 us: shards(): jnp.einsum('ijc,dc->ijd', tile_grad, proj_weight.astype(jnp.float32), pre...]
    reduce_scatter x1 -> x0, waiting for transfers between devices: 66.8 us -> none  [shards(): lax.psum_scatter(row_grad, 'col', scatter_dimension=1, tiled=True)]
    psum x1 -> x0, blocking collectives: 64.9 us -> none  [shards(): proj_grad = lax.psum(weight_part, ('row', 'col'))]
    pallas_call x0 -> x2, Pallas kernels: none -> 56.5 us  [the longest x1 51.2 us: band_pass(): pl.pallas_call(band_kernel, out_shape=(jax.ShapeDtypeStruct((GROUPS, 8, K...]
    convert_element_type x4 -> x0, other arithmetic: 20.2 us -> none  [the longest x1 14.3 us: norm_back(): (inv_scale * (scaled - first_mean - hatted * second_mean)).astype(jnp.bfl...]
    slice x31 -> x0, local copies, waits for them, and re-layouts: 20.2 us -> none  [the longest x17 12.6 us: shards(): cotangent = cot_all[lower:lower + QBLK] * valid_part[None, :, None]]
    reshape x3 -> x0, local copies, waits for them, and re-layouts: 14.9 us -> none  [the longest x1 9.84 us: shards(): tile_proj.astype(jnp.bfloat16).reshape(tok_rows, tok_cols * pair_width)]
    ppermute x6 -> x0, starting transfers between devices: 14.7 us -> none  [the longest x2 6.19 us: with_halo(): lax.ppermute(tail, axis, [(i, (i + 1) % count) for i in range(ends)])]
  transfers between devices with their start and end apart: 8 -> 0, of which waited for: 3 -> 0; matrix products, arithmetic and copies ran while one was open for 7% -> 0% of each run, Pallas kernels for 0% -> 0%
where the time goes in v2:
time: 57.5 us; the launch traced here: 57.2 us
  Pallas kernels  56.5 us (98%)
  between operations  0.64 us (1%)
    pallas_call x1, Pallas kernels, band_pass(): pl.pallas_call(band_kernel, out_shape=(jax.ShapeDtypeStruct((GROUPS, 8, K...  51.2 us
    pallas_call x1, Pallas kernels, place(): pl.pallas_call(place_kernel, out_shape=(jax.ShapeDtypeStruct((TOK, COLS,...  5.36 us

profile of v2, /device:TPU:0, one launch (start us, length us, event | category | flops | bytes accessed | tf_op | source)
XLA Modules:
  0.0 57.2 jit_solution(13199353359942641340)
XLA Ops:
  0.6 51.2 %band_pass.1 = (bf16[12,8,48,128]{3,2,1,0:T(8,128)(2,1)}, bf16[2,8,16,128]{3,2,1,0:T(8,128)(2,1)}, bf16[256,128]{1,0:T(8,128)(2,1)}, f32[16,128]{1,0:T(8,128)}) custom-call(s32[8]{0:T(128)} %start_ref.1, bf16[96,192,128]{2,1,0:T(8,128)(2,1)} %pair_ref.1, bf16[256,2048]{1,0:T(8,128)(2,1)} %cot_hbm.1, f32[1,128]{1,0:T(1,128)} %bitcast.8, ...), custom_call_target="tpu_custom_call" | custom-call | tf_op jit(solution)/shard_map/band_pass/pallas_call | solution.py:837
  51.8 5.4 %place.1 = (bf16[96,192,128]{2,1,0:T(8,128)(2,1)}, bf16[256,128]{1,0:T(8,128)(2,1)}, f32[16,128]{1,0:T(8,128)}) custom-call(bf16[12,8,48,128]{3,2,1,0:T(8,128)(2,1)} %get-tuple-element.10.grads_ref, bf16[2,8,16,128]{3,2,1,0:T(8,128)(2,1)} %get-tuple-element.11.corner_ref, bf16[256,128]{1,0:T(8,128)(2,1)} %get-tuple-element.12.atom_ref, ...), custom_call_target="tpu_custom_call" | custom-call | tf_op jit(solution)/shard_map/place/pallas_call | solution.py:1005

commit v3 on v2

--- a/solution.py
+++ b/solution.py
@@ -29,6 +29,18 @@
 QTOK = 32
 GROUPS = TOK // 8
 VMEM_LIMIT = 56 * 1024 * 1024
+MLP_ROWS = 1024
+NEAR = 19
+TOKEN_PART = (
+    (0, 40, 0, 384),
+    (0, 40, 0, 384),
+    (0, 32, 0, 512),
+    (8, 32, 0, 384),
+    (8, 32, 0, 384),
+    (0, 32, 0, 512),
+    (8, 40, 0, 384),
+    (8, 40, 128, 384),
+)
 
 
 def key_base(col):
@@ -68,6 +80,10 @@
 def dot_split(x, w):
     high, low = split(x)
     return dot(high, w) + dot(low, w)
+
+
+def dot_twice(x, w):
+    return dot(jnp.concatenate(split(x), axis=1), w)
 
 
 def sigmoid(x):
@@ -148,16 +164,29 @@
     return ahead, behind
 
 
-def tile_owners(row):
-    along_z = [4 * (row // 4) + lax.rem(row + step, 4) for step in range(1, 4)]
-    along_x = [lax.rem(row + 4 * step, N_ROW) for step in range(1, 4)]
-    return [(other, other // 2) for other in along_z], [(other, other // 2) for other in along_x]
+def like_places(row, col):
+    along_z = [(4 * (row // 4) + lax.rem(row + step, 4), col) for step in range(1, 4)]
+    along_x = [(lax.rem(row + 4 * step, N_ROW), col) for step in range(1, 4)]
+    return along_z, along_x
 
 
 def band_kernel(
     start_ref,
     pair_ref,
     cot_hbm,
+    gain_hbm,
+    proj_hbm,
+    feats_hbm,
+    counts_hbm,
+    query_w_hbm,
+    key_w_hbm,
+    first_w_hbm,
+    second_w_hbm,
+    third_w_hbm,
+    grads_hbm,
+    corner_grads_hbm,
+    atom_grad_ref,
+    proj_grad_ref,
     gain_ref,
     proj_ref,
     feats_ref,
@@ -167,25 +196,21 @@
     first_w_ref,
     second_w_ref,
     third_w_ref,
-    grads_ref,
-    corner_grads_ref,
-    atom_grad_ref,
-    proj_grad_ref,
+    grads,
+    corner_grads,
     band,
     corner_band,
-    flat,
-    corner_flat,
     zrow,
     zcorner,
     patch,
     patch_corner,
+    raw,
     feats_before,
     feats_after,
     counts_before,
     counts_after,
     cot_ref,
     act_ext,
-    lhs,
     rhs,
     query_high,
     query_low,
@@ -206,13 +231,14 @@
     patches,
     token_corner,
     tokens,
-    tokens_high,
-    tokens_low,
-    weight_part,
-    weight_corner,
+    near_flat,
+    near_high,
+    near_low,
+    weight_sent,
     weight_z,
     weight_x,
-    weight_total,
+    weight_row,
+    small_sems,
     load_sems,
     cot_sem,
     corner_load_sem,
@@ -220,6 +246,10 @@
     recv_z,
     send_c,
     recv_c,
+    send_r,
+    recv_r,
+    send_rc,
+    recv_rc,
     send_h,
     recv_h,
     send_t,
@@ -228,14 +258,12 @@
     recv_tc,
     send_k,
     recv_k,
-    send_wc,
-    recv_wc,
     send_wz,
     recv_wz,
     send_wx,
     recv_wx,
-    send_w,
-    recv_w,
+    send_wr,
+    recv_wr,
 ):
     row = lax.axis_index("row")
     col = lax.axis_index("col")
@@ -252,7 +280,8 @@
     other_device = holder != reader
     holder_col = jnp.clip(holder, 0, N_COL - 1)
     ahead, behind = neighbours(row, col)
-    along_z, along_x = tile_owners(row)
+    along_z, along_x = like_places(row, col)
+    along_row = [(row, lax.rem(col + step, N_COL)) for step in range(1, N_COL)]
 
     def remote(src, dst, send, recv, device):
         return pltpu.make_async_remote_copy(
@@ -264,6 +293,25 @@
             device_id_type=MESH,
         )
 
+    raw[...] = jnp.zeros_like(raw)
+
+    barrier = pltpu.get_barrier_semaphore()
+
+    def greet(device):
+        pl.semaphore_signal(barrier, inc=1, device_id=device, device_id_type=MESH)
+
+    @pl.when(col == 0)
+    def _():
+        greet(behind)
+
+    @pl.when(col == N_COL - 1)
+    def _():
+        greet(ahead)
+
+    for device in along_row + along_z + along_x:
+        greet(device)
+    greeted = N_COL - 1 + 6 + jnp.where((col == 0) | (col == N_COL - 1), 1, 0)
+
     def window_copy(group):
         first = pl.multiple_of(window_column(group, odd), 16)
         return pltpu.make_async_copy(
@@ -290,36 +338,26 @@
         corner_load.start()
 
     cot_load.start()
-
-    barrier = pltpu.get_barrier_semaphore()
-
-    def greet(device):
-        pl.semaphore_signal(barrier, inc=1, device_id=device, device_id_type=MESH)
-
-    greet(ahead)
-    greet(behind)
-
-    @pl.when(not_main)
-    def _():
-        greet((row, half))
-
-    @pl.when(is_main)
-    def _():
-        for step in range(1, N_COL):
-            greet((row, lax.rem(col + step, N_COL)))
-        for device in along_z + along_x:
-            greet(device)
-
-    @pl.when(is_holder & other_device)
-    def _():
-        greet((row, reader))
-
-    @pl.when(is_reader & other_device)
-    def _():
-        greet((row, holder_col))
-
-    greeted = 2 + jnp.where(is_main, N_COL - 1 + 6, 1)
-    greeted += jnp.where((is_holder | is_reader) & other_device, 1, 0)
+    smalls = [
+        pltpu.make_async_copy(src, dst, small_sems.at[at])
+        for at, (src, dst) in enumerate(
+            (
+                (gain_hbm, gain_ref),
+                (proj_hbm, proj_ref),
+                (feats_hbm, feats_ref),
+                (counts_hbm, counts_ref),
+                (query_w_hbm, query_w_ref),
+                (key_w_hbm, key_w_ref),
+                (first_w_hbm, first_w_ref),
+                (second_w_hbm, second_w_ref),
+                (third_w_hbm, third_w_ref),
+            )
+        )
+    ]
+    for copy in smalls:
+        copy.start()
+    for copy in smalls:
+        copy.wait()
 
     @pl.when(is_main)
     def _():
@@ -332,7 +370,6 @@
             hatted, _ = normalise(band[group])
             normed = (hatted * gain).astype(BF16)
             rows = jnp.concatenate([normed[i] for i in range(8)], axis=1)
-            flat[pl.ds(pl.multiple_of(KEYS * group, 16), KEYS), :] = rows
             at = pl.multiple_of(window_column(group, odd) - TOK * odd + 16, 16)
             lanes = pl.ds(pl.multiple_of(128 * group, 128), 128)
             zrow[pl.ds(at, KEYS), lanes] = dot(rows, spread_w).astype(BF16)
@@ -348,8 +385,23 @@
         normed = (hatted * gain_ref[...]).astype(BF16)
         for part in range(2):
             rows = jnp.concatenate([normed[8 * part + i] for i in range(8)], axis=1)
-            corner_flat[16 * part : 16 * part + 16, :] = rows
             zcorner[:, 128 * part : 128 * part + 128] = dot(rows, spread_w).astype(BF16)
+
+    cot_load.wait()
+
+    group = iota((16, 128), 1) // CA
+
+    def spread_step(eight, carry):
+        rows = cot_ref[pl.ds(pl.multiple_of(16 * eight, 16), 16), :].astype(F32)
+        for half in range(2):
+            at = pl.multiple_of(256 * eight + 128 * half, 128)
+            for chunk in range(16):
+                spread[pl.ds(at + 8 * chunk, 8), :] = rows[
+                    8 * half : 8 * half + 8, 128 * chunk : 128 * chunk + 128
+                ]
+        return carry
+
+    lax.fori_loop(0, ATOMS // 16, spread_step, 0, unroll=2)
 
     pl.semaphore_wait(barrier, greeted)
 
@@ -361,6 +413,40 @@
         return remote(src, patch, send_z.at[target], recv_z, (row, target))
 
     corner_copy = remote(zcorner, patch_corner, send_c, recv_c, (row, reader))
+
+    def raw_parts(target):
+        rows = pl.ds(11 * target, NEAR)
+        to_rows = pl.ds(11 * target - query_base_static(target), NEAR)
+        first = key_base(target)
+
+        def part(skip, width, parity):
+            src = pair_ref.at[rows, pl.ds(first + skip + TOK * parity, width)]
+            return src, raw.at[to_rows, pl.ds(skip, width)]
+
+        return [
+            (odd == parity, *part(16 if cut_low else 0, KEYS - 16 if cut_low or cut_high else KEYS, parity))
+            for parity in range(2)
+            for cut_low in (first + TOK * parity < 0,)
+            for cut_high in (first + TOK * parity + KEYS > COLS,)
+        ]
+
+    def for_raw(target, act):
+        for when, src, dst in raw_parts(target):
+
+            @pl.when(when & (col != target))
+            def _():
+                act(remote(src, dst, send_r.at[target], recv_r, (row, target)), True)
+
+            @pl.when(when & (col == target))
+            def _():
+                act(pltpu.make_async_copy(src, dst, recv_r), False)
+
+    raw_corner_src = pair_ref.at[
+        pl.ds(first_row, 16), pl.ds(pl.multiple_of(first_col, 16), 16)
+    ]
+    raw_corner_dst = raw.at[pl.ds(16 * odd, 16), pl.ds(pl.multiple_of(32 * odd, 16), 16)]
+    raw_corner_copy = remote(raw_corner_src, raw_corner_dst, send_rc, recv_rc, (row, reader))
+    raw_corner_local = pltpu.make_async_copy(raw_corner_src, raw_corner_dst, recv_rc)
 
     @pl.when(is_main)
     def _():
@@ -378,25 +464,32 @@
     @pl.when(is_holder & other_device)
     def _():
         corner_copy.start()
+        raw_corner_copy.start()
 
     @pl.when(is_holder & same_device)
     def _():
         patch_corner[...] = zcorner[...]
+        raw_corner_local.start()
 
     halos = [
         remote(src, dst, send_h.at[at], recv_h.at[at], device)
         for at, (src, dst, device) in enumerate(
             (
-                (feats_ref.at[pl.ds(ATOMS - HALO, HALO)], feats_before, ahead),
-                (feats_ref.at[pl.ds(0, HALO)], feats_after, behind),
-                (counts_ref, counts_before, ahead),
-                (counts_ref, counts_after, behind),
+                (feats_hbm.at[pl.ds(ATOMS - HALO, HALO)], feats_before, ahead),
+                (feats_hbm.at[pl.ds(0, HALO)], feats_after, behind),
+                (counts_hbm, counts_before, ahead),
+                (counts_hbm, counts_after, behind),
             )
         )
     ]
     for copy in halos:
         copy.start()
 
+    @pl.when(is_main)
+    def _():
+        for target in range(N_COL):
+            for_raw(target, lambda copy, far: copy.start())
+
     eye = channel_eye(LANES)
     eye16 = eye[:256]
     same = (iota((256, 256), 0) // CA) == (iota((256, 256), 1) // CA)
@@ -404,7 +497,8 @@
     def mixer(weight, flip):
         left = dot_nt(eye16, weight) if flip else dot(eye16, weight)
         wide = dot_nt(left.astype(BF16), eye16)
-        return jnp.where(same, wide, 0.0).astype(BF16)
+        wide = jnp.where(same, wide, 0.0).astype(BF16)
+        return jnp.concatenate([wide, wide], axis=0)
 
     mixers[0] = mixer(first_w_ref[...], False)
     mixers[1] = mixer(second_w_ref[...], False)
@@ -414,8 +508,8 @@
     key_tiled[...] = dot(eye, key_w_ref[...]).astype(BF16)
     query_tiled[...] = dot(eye, query_w_ref[...]).astype(BF16)
     eye_t = channel_eye_t(LANES)
-    rhs[128:256, :] = dot_tn(key_w_ref[...], eye_t).astype(BF16)
-    rhs[112:128, :] = jnp.zeros((16, LANES), BF16)
+    rhs[0:16, :] = jnp.zeros((16, LANES), BF16)
+    rhs[16:144, :] = dot_tn(key_w_ref[...], eye_t).astype(BF16)
 
     def activate(feats):
         floats = feats.astype(F32)
@@ -473,23 +567,7 @@
         hot_ref[block] = query_hot(block)
         return carry
 
-    lax.fori_loop(0, NBLK, hot_step, 0)
-
-    cot_load.wait()
-
-    group = iota((16, 128), 1) // CA
-
-    def spread_step(eight, carry):
-        rows = cot_ref[pl.ds(pl.multiple_of(16 * eight, 16), 16), :].astype(F32)
-        for half in range(2):
-            at = pl.multiple_of(256 * eight + 128 * half, 128)
-            for chunk in range(16):
-                spread[pl.ds(at + 8 * chunk, 8), :] = rows[
-                    8 * half : 8 * half + 8, 128 * chunk : 128 * chunk + 128
-                ]
-        return carry
-
-    lax.fori_loop(0, ATOMS // 16, spread_step, 0)
+    lax.fori_loop(0, NBLK, hot_step, 0, unroll=2)
 
     def swap_step(eight, carry):
         at = 128 * eight
@@ -500,7 +578,7 @@
             cot[pl.ds(to + key, 16, stride=8), :] = pieces[key]
         return carry
 
-    lax.fori_loop(0, ATOMS // 8, swap_step, 0)
+    lax.fori_loop(0, ATOMS // 8, swap_step, 0, unroll=4)
 
     for copy in halos:
         copy.wait()
@@ -562,16 +640,27 @@
         hot = hot_ref[block]
         window = start_ref[block] + block * QBLK + HALO
         atom = (iota((KWIN, 128), 0) + key_first(block)).astype(F32)
-        lhs[:, 0:128] = as_mask((lane_from <= atom) & (atom < lane_to))
-        lhs[:, 128:256] = act_ext[pl.ds(window, KWIN), :].astype(BF16)
-        rhs[0:48, :] = dot(patch[:, pl.ds(at, 256)], hot).astype(BF16)
-        mine = pl.multiple_of(block * QBLK, QBLK)
-        rhs[48:80, :] = query_high[pl.ds(mine, QBLK), :]
-        rhs[80:112, :] = query_low[pl.ds(mine, QBLK), :]
-        state[pl.ds(pl.multiple_of(block * KWIN, KWIN), KWIN), :] = dot(lhs[...], rhs[...])
+        mine = pl.ds(pl.multiple_of(block * QBLK, QBLK), QBLK)
+        left = jnp.concatenate(
+            [
+                as_mask((lane_from <= atom) & (atom < lane_to)),
+                act_ext[pl.ds(window, KWIN), :].astype(BF16),
+            ],
+            axis=1,
+        )
+        right = jnp.concatenate(
+            [
+                dot(patch[:, pl.ds(at, 256)], hot).astype(BF16),
+                query_high[mine, :],
+                query_low[mine, :],
+                rhs[...],
+            ],
+            axis=0,
+        )
+        state[pl.ds(pl.multiple_of(block * KWIN, KWIN), KWIN), :] = dot(left, right)
         return carry
 
-    lax.fori_loop(0, NBLK, start_step, 0)
+    lax.fori_loop(0, NBLK, start_step, 0, unroll=2)
 
     atom_low = jnp.where(row == 0, 0, -ROW_ATOMS)
     atom_high = jnp.where(row == N_ROW - 1, ROW_ATOMS, 2 * ROW_ATOMS)
@@ -580,33 +669,37 @@
         return sigma + act - act * sigma
 
     def mlp_step(step, carry):
-        pair = step // 2
-        at = pl.multiple_of(256 * pair, 256)
-        place = pl.ds(at, 256), pl.ds(pl.multiple_of(256 * (step % 2), 256), 256)
+        at = pl.multiple_of(MLP_ROWS * (step // 2), MLP_ROWS)
+        place = pl.ds(at, MLP_ROWS), pl.ds(pl.multiple_of(256 * (step % 2), 256), 256)
         value = state[place]
-        index = iota((256, 256), 0)
-        begin = jnp.where(index < KWIN, key_first(2 * pair), key_first(2 * pair + 1) - KWIN)
-        atom = index + begin
+        index = iota((KWIN, 256), 0)
+        atom = jnp.concatenate(
+            [
+                index + key_first(MLP_ROWS // KWIN * (step // 2) + block)
+                for block in range(MLP_ROWS // KWIN)
+            ],
+            axis=0,
+        )
         parts = [
-            cot[pl.ds(pl.multiple_of(at + NBLK * KWIN * (2 * (step % 2) + part), 256), 256), :]
+            cot[pl.ds(pl.multiple_of(at + NBLK * KWIN * (2 * (step % 2) + part), MLP_ROWS), MLP_ROWS), :]
             for part in range(2)
         ]
         grad = jnp.concatenate(parts, axis=1)
         grad = jnp.where((atom >= atom_low) & (atom < atom_high), grad, 0.0)
         sig_0 = sigmoid(value)
         act_0 = value * sig_0
-        one = dot_split(act_0, mixers[0])
+        one = dot_twice(act_0, mixers[0])
         sig_1 = sigmoid(one)
         act_1 = one * sig_1
-        two = dot_split(act_1, mixers[1])
+        two = dot_twice(act_1, mixers[1])
         sig_2 = sigmoid(two)
-        back = dot(grad.astype(BF16), mixers[2]) * slope(two, sig_2, two * sig_2)
-        back = dot_split(back, mixers[3]) * slope(one, sig_1, act_1)
-        back = dot_split(back, mixers[4]) * slope(value, sig_0, act_0)
+        back = dot(grad.astype(BF16), mixers[2, 0:256]) * slope(two, sig_2, two * sig_2)
+        back = dot_twice(back, mixers[3]) * slope(one, sig_1, act_1)
+        back = dot_twice(back, mixers[4]) * slope(value, sig_0, act_0)
         state[place] = grad + back
         return carry
 
-    lax.fori_loop(0, 8, mlp_step, 0)
+    lax.fori_loop(0, 2 * NBLK * KWIN // MLP_ROWS, mlp_step, 0)
 
     key_sum[...] = jnp.zeros_like(key_sum)
     token_sum[...] = jnp.zeros_like(token_sum)
@@ -637,23 +730,25 @@
         token_sum[:, pl.ds(at, 256)] += dot_nt(high, hot) + dot_nt(low, hot)
         return carry
 
-    lax.fori_loop(0, NBLK, sum_step, 0)
+    lax.fori_loop(0, NBLK, sum_step, 0, unroll=2)
 
     def token_copy(source):
-        return remote(token_sum, patches.at[source], send_t, recv_t.at[source], (row, half))
+        row_at, row_count, lane_at, lane_count = TOKEN_PART[source]
+        part = pl.ds(row_at, row_count), pl.ds(lane_at, lane_count)
+        return remote(
+            token_sum.at[part], patches.at[(source, *part)], send_t, recv_t.at[source], (row, half)
+        )
 
     corner_part = token_sum.at[
         pl.ds(pl.multiple_of(32 * odd, 16), 16), pl.ds(pl.multiple_of(256 * odd, 128), 256)
     ]
     token_corner_copy = remote(corner_part, token_corner, send_tc, recv_tc, (row, holder_col))
 
-    @pl.when(not_main)
-    def _():
-        token_copy(col).start()
-
-    @pl.when(is_main)
-    def _():
-        patches[col] = token_sum[...]
+    for source in range(N_COL):
+
+        @pl.when(not_main & (col == source))
+        def _():
+            token_copy(source).start()
 
     @pl.when(is_reader & other_device)
     def _():
@@ -675,121 +770,59 @@
     for copy in key_halos:
         copy.start()
 
-    def diagonal(wide):
-        total = wide[0:CA, 0:128]
-        for i in range(1, 8):
-            total += wide[CA * i : CA * i + CA, 128 * i : 128 * i + 128]
-        return total
-
-    def gradient(block, rows_high, rows_low, spread_w, gain):
-        hatted, inv_scale = normalise(block)
-        wide = dot(rows_high, spread_w) + dot(rows_low, spread_w)
-        scaled = jnp.stack([wide[:, 128 * i : 128 * i + 128] for i in range(8)]) * gain
-        first_mean = jnp.mean(scaled, axis=-1, keepdims=True)
-        second_mean = jnp.mean(scaled * hatted, axis=-1, keepdims=True)
-        return (inv_scale * (scaled - first_mean - hatted * second_mean)).astype(BF16)
-
-    corner_weight_copy = remote(
-        weight_part, weight_corner, send_wc, recv_wc, (row, half)
-    )
-
-    @pl.when(is_holder)
-    def _():
-        @pl.when(other_device)
-        def _():
-            token_corner_copy.wait_recv()
-
-        spread_w = spread_projection_t(proj_ref[...])
-        gain = gain_ref[...]
-        total = jnp.zeros((CA, CP), F32)
-        for part in range(2):
-            high, low = split(token_corner[:, 128 * part : 128 * part + 128])
-            rows = corner_flat[16 * part : 16 * part + 16, :]
-            total += diagonal(dot_tn(high, rows) + dot_tn(low, rows))
-        weight_part[...] = total
-        corner_weight_copy.start()
-        for part in range(2):
-            high, low = split(token_corner[:, 128 * part : 128 * part + 128])
-            corner_grads_ref[part] = gradient(
-                corner_band[8 * part : 8 * part + 8], high, low, spread_w, gain
-            )
-
+    @pl.when(is_main)
+    def _():
+        for target in range(N_COL):
+            for_raw(target, lambda copy, far: copy.wait_send() if far else copy.wait())
+
+    for target in range(N_COL):
+
+        for when, src, dst in raw_parts(target):
+
+            @pl.when(when & not_main & (col == target))
+            def _():
+                remote(src, dst, send_r.at[target], recv_r, (row, target)).wait_recv()
+
+    @pl.when(is_reader & other_device)
+    def _():
+        raw_corner_copy.wait_recv()
+
+    @pl.when(is_reader & same_device)
+    def _():
+        raw_corner_local.wait()
+
+    gain = gain_ref[...]
+
+    def near_step(eight, carry):
+        hatted, _ = normalise(raw[pl.ds(8 * eight, 8)])
+        normed = (hatted * gain).astype(BF16)
+        rows = pl.ds(pl.multiple_of(KEYS * eight, 16), KEYS)
+        near_flat[rows, :] = jnp.concatenate([normed[i] for i in range(8)], axis=1)
+        high, low = split(token_sum[:, pl.ds(pl.multiple_of(128 * eight, 128), 128)])
+        near_high[rows, :] = high
+        near_low[rows, :] = low
+        return carry
+
+    lax.fori_loop(0, QTOK // 8, near_step, 0)
+    wide = dot_tn(near_high[...], near_flat[...]) + dot_tn(near_low[...], near_flat[...])
+    weight = wide[0:CA, 0:128]
+    for i in range(1, 8):
+        weight += wide[CA * i : CA * i + CA, 128 * i : 128 * i + 128]
+    weight_sent[0] = weight
     z_copies = [
-        remote(weight_part, weight_z.at[at], send_wz.at[at], recv_wz.at[at], device)
+        remote(weight_sent.at[0], weight_z.at[at], send_wz.at[at], recv_wz.at[at], device)
         for at, device in enumerate(along_z)
     ]
     x_copies = [
-        remote(weight_total.at[0], weight_x.at[at], send_wx.at[at], recv_wx.at[at], device)
+        remote(weight_sent.at[1], weight_x.at[at], send_wx.at[at], recv_wx.at[at], device)
         for at, device in enumerate(along_x)
     ]
-
-    def total_copy(target):
-        return remote(
-            weight_total.at[1], weight_total.at[1], send_w.at[target], recv_w, (row, target)
-        )
-
-    @pl.when(is_main)
-    def _():
-        tokens[...] = jnp.zeros_like(tokens)
-        for source in range(N_COL):
-
-            @pl.when(col != source)
-            def _():
-                token_copy(source).wait_recv()
-
-            at = key_base(source) + 16
-            lanes = query_base_static(source) * CA
-            tokens[at : at + KEYS, lanes : lanes + QTOK * CA] += patches[source]
-
-        def cut(group, carry):
-            at = pl.multiple_of(window_column(group, odd) - TOK * odd + 16, 16)
-            lanes = pl.ds(pl.multiple_of(128 * group, 128), 128)
-            high, low = split(tokens[pl.ds(at, KEYS), lanes])
-            to = pl.ds(pl.multiple_of(KEYS * group, 16), KEYS)
-            tokens_high[to, :] = high
-            tokens_low[to, :] = low
-            return carry
-
-        lax.fori_loop(0, GROUPS, cut, 0)
-        total = diagonal(
-            dot_tn(tokens_high[...], flat[...]) + dot_tn(tokens_low[...], flat[...])
-        )
-
-        @pl.when(exists)
-        def _():
-            corner_weight_copy.wait_recv()
-
-        total += jnp.where(exists, weight_corner[...], 0.0)
-        weight_part[...] = total
-        for copy in z_copies:
-            copy.start()
-        spread_w = spread_projection_t(proj_ref[...])
-        gain = gain_ref[...]
-
-        def grad_step(group, carry):
-            rows = pl.ds(pl.multiple_of(KEYS * group, 16), KEYS)
-            grads_ref[group] = gradient(
-                band[group], tokens_high[rows, :], tokens_low[rows, :], spread_w, gain
-            )
-            return carry
-
-        lax.fori_loop(0, GROUPS // 2, grad_step, 0)
-        for at, copy in enumerate(z_copies):
-            copy.wait_recv()
-            total += weight_z[at]
-        weight_total[0] = total
-        for copy in x_copies:
-            copy.start()
-        lax.fori_loop(GROUPS // 2, GROUPS, grad_step, 0)
-        for at, copy in enumerate(x_copies):
-            copy.wait_recv()
-            total += weight_x[at]
-        weight_total[1] = total
-        for target in range(N_COL):
-
-            @pl.when(col != target)
-            def _():
-                total_copy(target).start()
+    row_copies = [
+        remote(weight_sent.at[2], weight_row.at[at], send_wr.at[at], recv_wr.at[at], device)
+        for at, device in enumerate(along_row)
+    ]
+    for copy in z_copies:
+        copy.start()
 
     for copy in key_halos:
         copy.wait()
@@ -801,33 +834,113 @@
     sigma = jax.nn.sigmoid(floats)
     atom_grad_ref[...] = (total * (sigma * (1.0 + floats * (1.0 - sigma)))).astype(BF16)
 
-    @pl.when(not_main)
-    def _():
-        token_copy(col).wait_send()
+    for at, copy in enumerate(z_copies):
+        copy.wait_recv()
+        weight += weight_z[at]
+    weight_sent[1] = weight
+    for copy in x_copies:
+        copy.start()
+
+    spread_wt = spread_projection_t(proj_ref[...])
+
+    def gradient(block, token_rows):
+        high, low = split(token_rows)
+        hatted, inv_scale = normalise(block)
+        wide = dot(high, spread_wt) + dot(low, spread_wt)
+        scaled = jnp.stack([wide[:, 128 * i : 128 * i + 128] for i in range(8)]) * gain
+        first_mean = jnp.mean(scaled, axis=-1, keepdims=True)
+        second_mean = jnp.mean(scaled * hatted, axis=-1, keepdims=True)
+        return (inv_scale * (scaled - first_mean - hatted * second_mean)).astype(BF16)
+
+    def grad_out(group):
+        return pltpu.make_async_copy(grads.at[group], grads_hbm.at[group], load_sems.at[group])
+
+    corner_out = pltpu.make_async_copy(corner_grads, corner_grads_hbm, corner_load_sem)
+
+    def grad_step(group, carry):
+        at = pl.multiple_of(window_column(group, odd) - TOK * odd + 16, 16)
+        lanes = pl.ds(pl.multiple_of(128 * group, 128), 128)
+        grads[group] = gradient(band[group], tokens[pl.ds(at, KEYS), lanes])
+        grad_out(group).start()
+        return carry
+
+    @pl.when(is_main)
+    def _():
+        tokens[...] = jnp.zeros_like(tokens)
+        for source in range(N_COL):
+            row_at, row_count, lane_at, lane_count = TOKEN_PART[source]
+            part = pl.ds(row_at, row_count), pl.ds(lane_at, lane_count)
+
+            @pl.when(col != source)
+            def _():
+                token_copy(source).wait_recv()
+
+            @pl.when(col == source)
+            def _():
+                patches[(source, *part)] = token_sum[part]
+
+            at = key_base(source) + 16 + row_at
+            lanes = query_base_static(source) * CA + lane_at
+            tokens[at : at + row_count, lanes : lanes + lane_count] += patches[(source, *part)]
+        lax.fori_loop(0, GROUPS // 2, grad_step, 0)
+
+    @pl.when(is_holder)
+    def _():
+        @pl.when(other_device)
+        def _():
+            token_corner_copy.wait_recv()
+
+        for part in range(2):
+            corner_grads[8 * part : 8 * part + 8] = gradient(
+                corner_band[8 * part : 8 * part + 8],
+                token_corner[:, 128 * part : 128 * part + 128],
+            )
+        corner_out.start()
+
+    for at, copy in enumerate(x_copies):
+        copy.wait_recv()
+        weight += weight_x[at]
+    weight_sent[2] = weight
+    for copy in row_copies:
+        copy.start()
+
+    @pl.when(is_main)
+    def _():
+        lax.fori_loop(GROUPS // 2, GROUPS, grad_step, 0)
+
+    for at, copy in enumerate(row_copies):
+        copy.wait_recv()
+        weight += weight_row[at]
+    proj_grad_ref[...] = weight
+
+    for copy in z_copies + x_copies + row_copies:
+        copy.wait_send()
+
+    for source in range(N_COL):
+
+        @pl.when(not_main & (col == source))
+        def _():
+            token_copy(source).wait_send()
 
     @pl.when(is_reader & other_device)
     def _():
         token_corner_copy.wait_send()
 
+    @pl.when(is_holder & other_device)
+    def _():
+        raw_corner_copy.wait_send()
+
+    @pl.when(is_main)
+    def _():
+        def grad_wait(group, carry):
+            grad_out(group).wait()
+            return carry
+
+        lax.fori_loop(0, GROUPS, grad_wait, 0)
+
     @pl.when(is_holder)
     def _():
-        corner_weight_copy.wait_send()
-
-    @pl.when(is_main)
-    def _():
-        for copy in z_copies + x_copies:
-            copy.wait_send()
-        for target in range(N_COL):
-
-            @pl.when(col != target)
-            def _():
-                total_copy(target).wait_send()
-
-    @pl.when(not_main)
-    def _():
-        total_copy(0).wait_recv()
-
-    proj_grad_ref[...] = weight_total[1]
+        corner_out.wait()
 
 
 def band_pass(start, pair_repr, cot, gain, proj, feats, counts, weights):
@@ -838,35 +951,44 @@
         band_kernel,
         out_shape=(
             jax.ShapeDtypeStruct((GROUPS, 8, KEYS, CP), BF16),
-            jax.ShapeDtypeStruct((2, 8, 16, CP), BF16),
+            jax.ShapeDtypeStruct((16, 16, CP), BF16),
             jax.ShapeDtypeStruct((ATOMS, CP), BF16),
             jax.ShapeDtypeStruct((CA, CP), F32),
         ),
-        in_specs=[pl.BlockSpec(memory_space=pltpu.SMEM), any_spec, any_spec] + [vmem] * 9,
-        out_specs=(vmem,) * 4,
+        in_specs=[pl.BlockSpec(memory_space=pltpu.SMEM)] + [any_spec] * 11,
+        out_specs=(any_spec, any_spec, vmem, vmem),
         scratch_shapes=[
+            pltpu.VMEM((1, CP), F32),
+            pltpu.VMEM((CA, CP), BF16),
+            pltpu.VMEM((ATOMS, CP), BF16),
+            pltpu.VMEM((1, TOK), jnp.int32),
+            pltpu.VMEM((CA, CP), BF16),
+            pltpu.VMEM((CA, CP), BF16),
+            pltpu.VMEM((CA, CA), BF16),
+            pltpu.VMEM((CA, CA), BF16),
+            pltpu.VMEM((CA, CA), BF16),
             pltpu.VMEM((GROUPS, 8, KEYS, CP), BF16),
             pltpu.VMEM((16, 16, CP), BF16),
-            pltpu.VMEM((GROUPS * KEYS, 8 * CP), BF16),
-            pltpu.VMEM((32, 8 * CP), BF16),
+            pltpu.VMEM((GROUPS, 8, KEYS, CP), BF16),
+            pltpu.VMEM((16, 16, CP), BF16),
             pltpu.VMEM((128, TOK * CA), BF16),
             pltpu.VMEM((16, 256), BF16),
             pltpu.VMEM((KEYS, QTOK * CA), BF16),
             pltpu.VMEM((16, 256), BF16),
+            pltpu.VMEM((QTOK, KEYS, CP), BF16),
             pltpu.VMEM((HALO, CP), BF16),
             pltpu.VMEM((HALO, CP), BF16),
             pltpu.VMEM((1, TOK), jnp.int32),
             pltpu.VMEM((1, TOK), jnp.int32),
             pltpu.VMEM((ATOMS, KWIN * CA), BF16),
             pltpu.VMEM((EXT, CP), F32),
-            pltpu.VMEM((KWIN, 256), BF16),
-            pltpu.VMEM((256, LANES), BF16),
+            pltpu.VMEM((144, LANES), BF16),
             pltpu.VMEM((ATOMS, LANES), BF16),
             pltpu.VMEM((ATOMS, LANES), BF16),
             pltpu.VMEM((ATOMS * 16, 128), F32),
             pltpu.VMEM((4 * NBLK * KWIN, 128), F32),
             pltpu.VMEM((NBLK * KWIN, LANES), F32),
-            pltpu.VMEM((5, 256, 256), BF16),
+            pltpu.VMEM((5, 512, 256), BF16),
             pltpu.VMEM((LANES, CP), BF16),
             pltpu.VMEM((LANES, CP), BF16),
             pltpu.VMEM((LANES, 128), F32),
@@ -880,14 +1002,19 @@
             pltpu.VMEM((N_COL, KEYS, QTOK * CA), F32),
             pltpu.VMEM((16, 256), F32),
             pltpu.VMEM((128, TOK * CA), F32),
-            pltpu.VMEM((GROUPS * KEYS, 128), BF16),
-            pltpu.VMEM((GROUPS * KEYS, 128), BF16),
-            pltpu.VMEM((CA, CP), F32),
-            pltpu.VMEM((CA, CP), F32),
+            pltpu.VMEM((QTOK // 8 * KEYS, 8 * CP), BF16),
+            pltpu.VMEM((QTOK // 8 * KEYS, 128), BF16),
+            pltpu.VMEM((QTOK // 8 * KEYS, 128), BF16),
             pltpu.VMEM((3, CA, CP), F32),
             pltpu.VMEM((3, CA, CP), F32),
-            pltpu.VMEM((2, CA, CP), F32),
+            pltpu.VMEM((3, CA, CP), F32),
+            pltpu.VMEM((N_COL - 1, CA, CP), F32),
+            dma((9,)),
             dma((GROUPS,)),
+            dma,
+            dma,
+            dma((N_COL,)),
+            dma,
             dma,
             dma,
             dma((N_COL,)),
@@ -902,14 +1029,12 @@
             dma,
             dma((2,)),
             dma((2,)),
-            dma,
-            dma,
             dma((3,)),
             dma((3,)),
             dma((3,)),
             dma((3,)),
-            dma((N_COL,)),
-            dma,
+            dma((N_COL - 1,)),
+            dma((N_COL - 1,)),
         ],
         compiler_params=pltpu.CompilerParams(
             collective_id=0, has_side_effects=True, vmem_limit_bytes=VMEM_LIMIT
@@ -926,11 +1051,9 @@
     pair_grad_ref,
     atom_grad_ref,
     proj_grad_ref,
-    rows,
     zeros,
-    load_sems,
-    corner_sem,
-    store_sems,
+    held,
+    sems,
 ):
     row = lax.axis_index("row")
     col = lax.axis_index("col")
@@ -939,64 +1062,62 @@
     is_main = col == half
     holder = jnp.where(odd == 0, half - 1, half + 1)
     is_holder = col == holder
-    plain = (col != half) & (col != holder)
-
-    def load(group):
-        first = pl.multiple_of(window_column(group, odd), 16)
+    zeros[...] = jnp.zeros_like(zeros)
+
+    def blank(group, first, last, sem):
         return pltpu.make_async_copy(
-            grads_ref.at[group], rows.at[group, :, pl.ds(first, KEYS)], load_sems.at[group]
+            zeros.at[:, pl.ds(0, last - first)],
+            pair_grad_ref.at[pl.ds(8 * group, 8), pl.ds(first, last - first)],
+            sem,
         )
 
-    def store(group, source):
-        return pltpu.make_async_copy(
-            source, pair_grad_ref.at[pl.ds(8 * group, 8)], store_sems.at[group]
-        )
-
-    @pl.when(is_main)
-    def _():
-        rows[...] = jnp.zeros_like(rows)
+    def pieces(kind, parity):
+        copies, loads, stores = [], [], []
         for group in range(GROUPS):
-            load(group).start()
-        for group in range(GROUPS):
-            load(group).wait()
-            store(group, rows.at[group]).start()
-
-    zeros[...] = jnp.zeros_like(zeros)
-
-    @pl.when(is_holder)
-    def _():
-        first_row, first_col = corner_place(odd)
-        rows[0:2] = jnp.zeros((2, 8, COLS, CP), BF16)
-        copy = pltpu.make_async_copy(
-            corner_ref,
-            rows.at[pl.ds(0, 2), :, pl.ds(pl.multiple_of(first_col, 16), 16)],
-            corner_sem,
-        )
-        copy.start()
-        for group in range(2, GROUPS - 2):
-            store(group, zeros).start()
-        copy.wait()
-        for part in range(2):
-
-            @pl.when(odd == 0)
-            def _():
-                store(part, rows.at[part]).start()
-                store(GROUPS - 2 + part, zeros).start()
-
-            @pl.when(odd == 1)
-            def _():
-                store(part, zeros).start()
-                store(GROUPS - 2 + part, rows.at[part]).start()
-
-    @pl.when(plain)
-    def _():
-        for group in range(GROUPS):
-            store(group, zeros).start()
+            first, last, source = 0, 0, None
+            if kind == "band":
+                first = 16 * ((8 * group - 13 + 16) // 16) - 16 + TOK * parity
+                first = min(max(first, 0), COLS - KEYS)
+                last, source = first + KEYS, (grads_ref.at[group], held.at[group])
+            elif kind == "corner" and group // 2 == 5 * parity:
+                first = 176 * (1 - parity)
+                last = first + 16
+                source = (
+                    corner_ref.at[pl.ds(8 * (group % 2), 8)],
+                    held.at[group, :, pl.ds(0, 16)],
+                )
+            if source is not None:
+                to = pair_grad_ref.at[pl.ds(8 * group, 8), pl.ds(first, last - first)]
+                loads.append(pltpu.make_async_copy(*source, sems.at[group, 0]))
+                stores.append(pltpu.make_async_copy(source[1], to, sems.at[group, 3]))
+            if first > 0:
+                copies.append(blank(group, 0, first, sems.at[group, 1]))
+            if last < COLS:
+                copies.append(blank(group, last, COLS, sems.at[group, 2]))
+        return copies, loads, stores
+
+    cases = (
+        (is_main & (odd == 0), "band", 0),
+        (is_main & (odd == 1), "band", 1),
+        (is_holder & (odd == 0), "corner", 0),
+        (is_holder & (odd == 1), "corner", 1),
+        (jnp.logical_not(is_main | is_holder), "none", 0),
+    )
+    for when, kind, parity in cases:
+
+        @pl.when(when)
+        def _():
+            copies, loads, stores = pieces(kind, parity)
+            for copy in loads + copies:
+                copy.start()
+            for load, store in zip(loads, stores):
+                load.wait()
+                store.start()
+            for copy in copies + stores:
+                copy.wait()
 
     atom_grad_ref[...] = atom_ref[...]
     proj_grad_ref[...] = proj_ref[...]
-    for group in range(GROUPS):
-        store(group, zeros).wait()
 
 
 def place(grads, corner, atom_grad, proj_grad):
@@ -1012,11 +1133,9 @@
         in_specs=[any_spec, any_spec, vmem, vmem],
         out_specs=(any_spec, vmem, vmem),
         scratch_shapes=[
-            pltpu.VMEM((GROUPS, 8, COLS, CP), BF16),
             pltpu.VMEM((8, COLS, CP), BF16),
-            pltpu.SemaphoreType.DMA((GROUPS,)),
-            pltpu.SemaphoreType.DMA,
-            pltpu.SemaphoreType.DMA((GROUPS,)),
+            pltpu.VMEM((GROUPS, 8, KEYS, CP), BF16),
+            pltpu.SemaphoreType.DMA((GROUPS, 4)),
         ],
         compiler_params=pltpu.CompilerParams(vmem_limit_bytes=VMEM_LIMIT),
         name="place",

time: 57.5 us -> 46 us (0.80)
  Pallas kernels: 56.5 us -> 45 us
    pallas_call x1, Pallas kernels: 51.2 us -> 40.1 us  [band_pass(): pl.pallas_call(band_kernel, out_shape=(jax.ShapeDtypeStruct((GROUPS, 8, K...]
where the time goes in v3:
time: 46 us; the launch traced here: 45.7 us
  Pallas kernels  45 us (98%)
  between operations  0.64 us (1%)
    pallas_call x1, Pallas kernels, band_pass(): pl.pallas_call(band_kernel, out_shape=(jax.ShapeDtypeStruct((GROUPS, 8, K...  40.1 us
    pallas_call x1, Pallas kernels, place(): pl.pallas_call(place_kernel, out_shape=(jax.ShapeDtypeStruct((TOK, COLS,...  4.99 us

profile of v3, /device:TPU:0, one launch (start us, length us, event | category | flops | bytes accessed | tf_op | source)
XLA Modules:
  0.0 45.7 jit_solution(13317919774772710633)
XLA Ops:
  0.6 40.1 %band_pass.1 = (bf16[12,8,48,128]{3,2,1,0:T(8,128)(2,1)}, bf16[16,16,128]{2,1,0:T(8,128)(2,1)}, bf16[256,128]{1,0:T(8,128)(2,1)}, f32[16,128]{1,0:T(8,128)}) custom-call(s32[8]{0:T(128)} %start_ref.1, bf16[96,192,128]{2,1,0:T(8,128)(2,1)} %pair_ref.1, bf16[256,2048]{1,0:T(8,128)(2,1)} %cot_hbm.1, f32[1,128]{1,0:T(1,128)} %bitcast.8, ...), custom_call_target="tpu_custom_call" | custom-call | tf_op jit(solution)/shard_map/band_pass/pallas_call | solution.py:950
  40.7 5.0 %place.1 = (bf16[96,192,128]{2,1,0:T(8,128)(2,1)}, bf16[256,128]{1,0:T(8,128)(2,1)}, f32[16,128]{1,0:T(8,128)}) custom-call(bf16[12,8,48,128]{3,2,1,0:T(8,128)(2,1)} %get-tuple-element.10.grads_ref, bf16[16,16,128]{2,1,0:T(8,128)(2,1)} %get-tuple-element.11.corner_ref, bf16[256,128]{1,0:T(8,128)(2,1)} %get-tuple-element.12.atom_ref, ...), custom_call_target="tpu_custom_call" | custom-call | tf_op jit(solution)/shard_map/place/pallas_call | solution.py:1126

commit v4 on v3

--- a/solution.py
+++ b/solution.py
@@ -165,9 +165,7 @@
 
 
 def like_places(row, col):
-    along_z = [(4 * (row // 4) + lax.rem(row + step, 4), col) for step in range(1, 4)]
-    along_x = [(lax.rem(row + 4 * step, N_ROW), col) for step in range(1, 4)]
-    return along_z, along_x
+    return [(lax.rem(row + step, N_ROW), col) for step in range(1, N_ROW)]
 
 
 def band_kernel(
@@ -235,9 +233,8 @@
     near_high,
     near_low,
     weight_sent,
-    weight_z,
-    weight_x,
     weight_row,
+    weight_grid,
     small_sems,
     load_sems,
     cot_sem,
@@ -258,12 +255,10 @@
     recv_tc,
     send_k,
     recv_k,
-    send_wz,
-    recv_wz,
-    send_wx,
-    recv_wx,
     send_wr,
     recv_wr,
+    send_wg,
+    recv_wg,
 ):
     row = lax.axis_index("row")
     col = lax.axis_index("col")
@@ -280,7 +275,7 @@
     other_device = holder != reader
     holder_col = jnp.clip(holder, 0, N_COL - 1)
     ahead, behind = neighbours(row, col)
-    along_z, along_x = like_places(row, col)
+    along_grid = like_places(row, col)
     along_row = [(row, lax.rem(col + step, N_COL)) for step in range(1, N_COL)]
 
     def remote(src, dst, send, recv, device):
@@ -308,9 +303,9 @@
     def _():
         greet(ahead)
 
-    for device in along_row + along_z + along_x:
+    for device in along_row + along_grid:
         greet(device)
-    greeted = N_COL - 1 + 6 + jnp.where((col == 0) | (col == N_COL - 1), 1, 0)
+    greeted = N_COL + N_ROW - 2 + jnp.where((col == 0) | (col == N_COL - 1), 1, 0)
 
     def window_copy(group):
         first = pl.multiple_of(window_column(group, odd), 16)
@@ -809,20 +804,82 @@
     for i in range(1, 8):
         weight += wide[CA * i : CA * i + CA, 128 * i : 128 * i + 128]
     weight_sent[0] = weight
-    z_copies = [
-        remote(weight_sent.at[0], weight_z.at[at], send_wz.at[at], recv_wz.at[at], device)
-        for at, device in enumerate(along_z)
-    ]
-    x_copies = [
-        remote(weight_sent.at[1], weight_x.at[at], send_wx.at[at], recv_wx.at[at], device)
-        for at, device in enumerate(along_x)
-    ]
     row_copies = [
-        remote(weight_sent.at[2], weight_row.at[at], send_wr.at[at], recv_wr.at[at], device)
+        remote(weight_sent.at[0], weight_row.at[at], send_wr.at[at], recv_wr.at[at], device)
         for at, device in enumerate(along_row)
     ]
-    for copy in z_copies:
+    grid_copies = [
+        remote(weight_sent.at[1], weight_grid.at[at], send_wg.at[at], recv_wg.at[at], device)
+        for at, device in enumerate(along_grid)
+    ]
+    for copy in row_copies:
         copy.start()
+    for at, copy in enumerate(row_copies):
+        copy.wait_recv()
+        weight += weight_row[at]
+    weight_sent[1] = weight
+    for copy in grid_copies:
+        copy.start()
+
+    spread_wt = spread_projection_t(proj_ref[...])
+
+    def gradient(block, token_rows):
+        high, low = split(token_rows)
+        hatted, inv_scale = normalise(block)
+        wide = dot(high, spread_wt) + dot(low, spread_wt)
+        scaled = jnp.stack([wide[:, 128 * i : 128 * i + 128] for i in range(8)]) * gain
+        first_mean = jnp.mean(scaled, axis=-1, keepdims=True)
+        second_mean = jnp.mean(scaled * hatted, axis=-1, keepdims=True)
+        return (inv_scale * (scaled - first_mean - hatted * second_mean)).astype(BF16)
+
+    def grad_out(group):
+        return pltpu.make_async_copy(grads.at[group], grads_hbm.at[group], load_sems.at[group])
+
+    corner_out = pltpu.make_async_copy(corner_grads, corner_grads_hbm, corner_load_sem)
+
+    def grad_step(group, carry):
+        at = pl.multiple_of(window_column(group, odd) - TOK * odd + 16, 16)
+        lanes = pl.ds(pl.multiple_of(128 * group, 128), 128)
+        grads[group] = gradient(band[group], tokens[pl.ds(at, KEYS), lanes])
+        grad_out(group).start()
+        return carry
+
+    @pl.when(is_main)
+    def _():
+        tokens[...] = jnp.zeros_like(tokens)
+        for source in range(N_COL):
+            row_at, row_count, lane_at, lane_count = TOKEN_PART[source]
+            part = pl.ds(row_at, row_count), pl.ds(lane_at, lane_count)
+
+            @pl.when(col != source)
+            def _():
+                token_copy(source).wait_recv()
+
+            @pl.when(col == source)
+            def _():
+                patches[(source, *part)] = token_sum[part]
+
+            at = key_base(source) + 16 + row_at
+            lanes = query_base_static(source) * CA + lane_at
+            tokens[at : at + row_count, lanes : lanes + lane_count] += patches[(source, *part)]
+        lax.fori_loop(0, GROUPS // 2, grad_step, 0)
+
+    @pl.when(is_holder)
+    def _():
+        @pl.when(other_device)
+        def _():
+            token_corner_copy.wait_recv()
+
+        for part in range(2):
+            corner_grads[8 * part : 8 * part + 8] = gradient(
+                corner_band[8 * part : 8 * part + 8],
+                token_corner[:, 128 * part : 128 * part + 128],
+            )
+        corner_out.start()
+
+    @pl.when(is_main)
+    def _():
+        lax.fori_loop(GROUPS // 2, GROUPS, grad_step, 0)
 
     for copy in key_halos:
         copy.wait()
@@ -834,86 +891,12 @@
     sigma = jax.nn.sigmoid(floats)
     atom_grad_ref[...] = (total * (sigma * (1.0 + floats * (1.0 - sigma)))).astype(BF16)
 
-    for at, copy in enumerate(z_copies):
+    for at, copy in enumerate(grid_copies):
         copy.wait_recv()
-        weight += weight_z[at]
-    weight_sent[1] = weight
-    for copy in x_copies:
-        copy.start()
-
-    spread_wt = spread_projection_t(proj_ref[...])
-
-    def gradient(block, token_rows):
-        high, low = split(token_rows)
-        hatted, inv_scale = normalise(block)
-        wide = dot(high, spread_wt) + dot(low, spread_wt)
-        scaled = jnp.stack([wide[:, 128 * i : 128 * i + 128] for i in range(8)]) * gain
-        first_mean = jnp.mean(scaled, axis=-1, keepdims=True)
-        second_mean = jnp.mean(scaled * hatted, axis=-1, keepdims=True)
-        return (inv_scale * (scaled - first_mean - hatted * second_mean)).astype(BF16)
-
-    def grad_out(group):
-        return pltpu.make_async_copy(grads.at[group], grads_hbm.at[group], load_sems.at[group])
-
-    corner_out = pltpu.make_async_copy(corner_grads, corner_grads_hbm, corner_load_sem)
-
-    def grad_step(group, carry):
-        at = pl.multiple_of(window_column(group, odd) - TOK * odd + 16, 16)
-        lanes = pl.ds(pl.multiple_of(128 * group, 128), 128)
-        grads[group] = gradient(band[group], tokens[pl.ds(at, KEYS), lanes])
-        grad_out(group).start()
-        return carry
-
-    @pl.when(is_main)
-    def _():
-        tokens[...] = jnp.zeros_like(tokens)
-        for source in range(N_COL):
-            row_at, row_count, lane_at, lane_count = TOKEN_PART[source]
-            part = pl.ds(row_at, row_count), pl.ds(lane_at, lane_count)
-
-            @pl.when(col != source)
-            def _():
-                token_copy(source).wait_recv()
-
-            @pl.when(col == source)
-            def _():
-                patches[(source, *part)] = token_sum[part]
-
-            at = key_base(source) + 16 + row_at
-            lanes = query_base_static(source) * CA + lane_at
-            tokens[at : at + row_count, lanes : lanes + lane_count] += patches[(source, *part)]
-        lax.fori_loop(0, GROUPS // 2, grad_step, 0)
-
-    @pl.when(is_holder)
-    def _():
-        @pl.when(other_device)
-        def _():
-            token_corner_copy.wait_recv()
-
-        for part in range(2):
-            corner_grads[8 * part : 8 * part + 8] = gradient(
-                corner_band[8 * part : 8 * part + 8],
-                token_corner[:, 128 * part : 128 * part + 128],
-            )
-        corner_out.start()
-
-    for at, copy in enumerate(x_copies):
-        copy.wait_recv()
-        weight += weight_x[at]
-    weight_sent[2] = weight
-    for copy in row_copies:
-        copy.start()
-
-    @pl.when(is_main)
-    def _():
-        lax.fori_loop(GROUPS // 2, GROUPS, grad_step, 0)
-
-    for at, copy in enumerate(row_copies):
-        copy.wait_recv()
-        weight += weight_row[at]
+        weight += weight_grid[at]
     proj_grad_ref[...] = weight
 
-    for copy in z_copies + x_copies + row_copies:
+    for copy in row_copies + grid_copies:
         copy.wait_send()
 
     for source in range(N_COL):
@@ -1005,10 +988,9 @@
             pltpu.VMEM((QTOK // 8 * KEYS, 8 * CP), BF16),
             pltpu.VMEM((QTOK // 8 * KEYS, 128), BF16),
             pltpu.VMEM((QTOK // 8 * KEYS, 128), BF16),
-            pltpu.VMEM((3, CA, CP), F32),
-            pltpu.VMEM((3, CA, CP), F32),
-            pltpu.VMEM((3, CA, CP), F32),
+            pltpu.VMEM((2, CA, CP), F32),
             pltpu.VMEM((N_COL - 1, CA, CP), F32),
+            pltpu.VMEM((N_ROW - 1, CA, CP), F32),
             dma((9,)),
             dma((GROUPS,)),
             dma,
@@ -1029,12 +1011,10 @@
             dma,
             dma((2,)),
             dma((2,)),
-            dma((3,)),
-            dma((3,)),
-            dma((3,)),
-            dma((3,)),
             dma((N_COL - 1,)),
             dma((N_COL - 1,)),
+            dma((N_ROW - 1,)),
+            dma((N_ROW - 1,)),
         ],
         compiler_params=pltpu.CompilerParams(
             collective_id=0, has_side_effects=True, vmem_limit_bytes=VMEM_LIMIT

time: 46 us -> 45 us (0.978)
  Pallas kernels: 45 us -> 44.1 us
    pallas_call x1, Pallas kernels: 40.1 us -> 39.1 us  [band_pass(): pl.pallas_call(band_kernel, out_shape=(jax.ShapeDtypeStruct((GROUPS, 8, K...]
where the time goes in v4:
time: 45 us; the launch traced here: 44.8 us
  Pallas kernels  44.1 us (98%)
  between operations  0.64 us (1%)
    pallas_call x1, Pallas kernels, band_pass(): pl.pallas_call(band_kernel, out_shape=(jax.ShapeDtypeStruct((GROUPS, 8, K...  39.1 us
    pallas_call x1, Pallas kernels, place(): pl.pallas_call(place_kernel, out_shape=(jax.ShapeDtypeStruct((TOK, COLS,...  4.99 us

profile of v4, /device:TPU:0, one launch (start us, length us, event | category | flops | bytes accessed | tf_op | source)
XLA Modules:
  0.0 44.8 jit_solution(7201418812309904287)
XLA Ops:
  0.6 39.1 %band_pass.1 = (bf16[12,8,48,128]{3,2,1,0:T(8,128)(2,1)}, bf16[16,16,128]{2,1,0:T(8,128)(2,1)}, bf16[256,128]{1,0:T(8,128)(2,1)}, f32[16,128]{1,0:T(8,128)}) custom-call(s32[8]{0:T(128)} %start_ref.1, bf16[96,192,128]{2,1,0:T(8,128)(2,1)} %pair_ref.1, bf16[256,2048]{1,0:T(8,128)(2,1)} %cot_hbm.1, f32[1,128]{1,0:T(1,128)} %bitcast.8, ...), custom_call_target="tpu_custom_call" | custom-call | tf_op jit(solution)/shard_map/band_pass/pallas_call | solution.py:933
  39.8 5.0 %place.1 = (bf16[96,192,128]{2,1,0:T(8,128)(2,1)}, bf16[256,128]{1,0:T(8,128)(2,1)}, f32[16,128]{1,0:T(8,128)}) custom-call(bf16[12,8,48,128]{3,2,1,0:T(8,128)(2,1)} %get-tuple-element.10.grads_ref, bf16[16,16,128]{2,1,0:T(8,128)(2,1)} %get-tuple-element.11.corner_ref, bf16[256,128]{1,0:T(8,128)(2,1)} %get-tuple-element.12.atom_ref, ...), custom_call_target="tpu_custom_call" | custom-call | tf_op jit(solution)/shard_map/place/pallas_call | solution.py:1106

commit v5 on v4

--- a/solution.py
+++ b/solution.py
@@ -477,8 +477,16 @@
             )
         )
     ]
-    for copy in halos:
-        copy.start()
+    halos[0].start()
+    halos[1].start()
+
+    @pl.when(col == N_COL - 1)
+    def _():
+        halos[2].start()
+
+    @pl.when(col == 0)
+    def _():
+        halos[3].start()
 
     @pl.when(is_main)
     def _():
@@ -575,14 +583,25 @@
 
     lax.fori_loop(0, ATOMS // 8, swap_step, 0, unroll=4)
 
-    for copy in halos:
-        copy.wait()
+    halos[0].wait()
+    halos[1].wait()
+
+    @pl.when(col == N_COL - 1)
+    def _():
+        halos[2].wait_send()
+        halos[3].wait_recv()
+
+    @pl.when(col == 0)
+    def _():
+        halos[3].wait_send()
+        halos[2].wait_recv()
+
     act_ext[0:HALO] = activate(feats_before[...])
     act_ext[HALO + ATOMS : EXT] = activate(feats_after[...])
 
     base = key_base(col)
-    before = counts_before[...].astype(F32)
-    after = counts_after[...].astype(F32)
+    before = jnp.where(col == 0, counts_before[...], counts_ref[...]).astype(F32)
+    after = jnp.where(col == N_COL - 1, counts_after[...], counts_ref[...]).astype(F32)
 
     def lane_bounds(offset):
         token = iota((TOK, 128), 1) + (base + offset)
@@ -689,8 +708,8 @@
         two = dot_twice(act_1, mixers[1])
         sig_2 = sigmoid(two)
         back = dot(grad.astype(BF16), mixers[2, 0:256]) * slope(two, sig_2, two * sig_2)
-        back = dot_twice(back, mixers[3]) * slope(one, sig_1, act_1)
-        back = dot_twice(back, mixers[4]) * slope(value, sig_0, act_0)
+        back = dot(back.astype(BF16), mixers[3, 0:256]) * slope(one, sig_1, act_1)
+        back = dot(back.astype(BF16), mixers[4, 0:256]) * slope(value, sig_0, act_0)
         state[place] = grad + back
         return carry
 

time: 45 us -> 44.1 us (0.980)
  Pallas kernels: 44.1 us -> 43.2 us
    pallas_call x1, Pallas kernels: 39.1 us -> 38.2 us  [band_pass(): pl.pallas_call(band_kernel, out_shape=(jax.ShapeDtypeStruct((GROUPS, 8, K...]
where the time goes in v5:
time: 44.1 us; the launch traced here: 43.8 us
  Pallas kernels  43.2 us (98%)
  between operations  0.64 us (1%)
    pallas_call x1, Pallas kernels, band_pass(): pl.pallas_call(band_kernel, out_shape=(jax.ShapeDtypeStruct((GROUPS, 8, K...  38.2 us
    pallas_call x1, Pallas kernels, place(): pl.pallas_call(place_kernel, out_shape=(jax.ShapeDtypeStruct((TOK, COLS,...  4.99 us

profile of v5, /device:TPU:0, one launch (start us, length us, event | category | flops | bytes accessed | tf_op | source)
XLA Modules:
  0.0 43.8 jit_solution(16517498985765994970)
XLA Ops:
  0.6 38.2 %band_pass.1 = (bf16[12,8,48,128]{3,2,1,0:T(8,128)(2,1)}, bf16[16,16,128]{2,1,0:T(8,128)(2,1)}, bf16[256,128]{1,0:T(8,128)(2,1)}, f32[16,128]{1,0:T(8,128)}) custom-call(s32[8]{0:T(128)} %start_ref.1, bf16[96,192,128]{2,1,0:T(8,128)(2,1)} %pair_ref.1, bf16[256,2048]{1,0:T(8,128)(2,1)} %cot_hbm.1, f32[1,128]{1,0:T(1,128)} %bitcast.8, ...), custom_call_target="tpu_custom_call" | custom-call | tf_op jit(solution)/shard_map/band_pass/pallas_call | solution.py:952
  38.8 5.0 %place.1 = (bf16[96,192,128]{2,1,0:T(8,128)(2,1)}, bf16[256,128]{1,0:T(8,128)(2,1)}, f32[16,128]{1,0:T(8,128)}) custom-call(bf16[12,8,48,128]{3,2,1,0:T(8,128)(2,1)} %get-tuple-element.10.grads_ref, bf16[16,16,128]{2,1,0:T(8,128)(2,1)} %get-tuple-element.11.corner_ref, bf16[256,128]{1,0:T(8,128)(2,1)} %get-tuple-element.12.atom_ref, ...), custom_call_target="tpu_custom_call" | custom-call | tf_op jit(solution)/shard_map/place/pallas_call | solution.py:1125

commit v6 on v5

--- a/solution.py
+++ b/solution.py
@@ -817,7 +817,7 @@
         near_low[rows, :] = low
         return carry
 
-    lax.fori_loop(0, QTOK // 8, near_step, 0)
+    lax.fori_loop(0, QTOK // 8, near_step, 0, unroll=2)
     wide = dot_tn(near_high[...], near_flat[...]) + dot_tn(near_low[...], near_flat[...])
     weight = wide[0:CA, 0:128]
     for i in range(1, 8):
@@ -881,7 +881,7 @@
             at = key_base(source) + 16 + row_at
             lanes = query_base_static(source) * CA + lane_at
             tokens[at : at + row_count, lanes : lanes + lane_count] += patches[(source, *part)]
-        lax.fori_loop(0, GROUPS // 2, grad_step, 0)
+        lax.fori_loop(0, GROUPS // 2, grad_step, 0, unroll=2)
 
     @pl.when(is_holder)
     def _():
@@ -898,7 +898,7 @@
 
     @pl.when(is_main)
     def _():
-        lax.fori_loop(GROUPS // 2, GROUPS, grad_step, 0)
+        lax.fori_loop(GROUPS // 2, GROUPS, grad_step, 0, unroll=2)
 
     for copy in key_halos:
         copy.wait()

time: 44.1 us -> 43.9 us (level)
  no operation moved by 1% of the time
where the time goes in v6:
time: 43.9 us; the launch traced here: 43.6 us
  Pallas kernels  43 us (98%)
  between operations  0.64 us (1%)
    pallas_call x1, Pallas kernels, band_pass(): pl.pallas_call(band_kernel, out_shape=(jax.ShapeDtypeStruct((GROUPS, 8, K...  38 us
    pallas_call x1, Pallas kernels, place(): pl.pallas_call(place_kernel, out_shape=(jax.ShapeDtypeStruct((TOK, COLS,...  4.99 us

profile of v6, /device:TPU:0, one launch (start us, length us, event | category | flops | bytes accessed | tf_op | source)
XLA Modules:
  0.0 43.6 jit_solution(17563585481982407845)
XLA Ops:
  0.6 38.0 %band_pass.1 = (bf16[12,8,48,128]{3,2,1,0:T(8,128)(2,1)}, bf16[16,16,128]{2,1,0:T(8,128)(2,1)}, bf16[256,128]{1,0:T(8,128)(2,1)}, f32[16,128]{1,0:T(8,128)}) custom-call(s32[8]{0:T(128)} %start_ref.1, bf16[96,192,128]{2,1,0:T(8,128)(2,1)} %pair_ref.1, bf16[256,2048]{1,0:T(8,128)(2,1)} %cot_hbm.1, f32[1,128]{1,0:T(1,128)} %bitcast.8, ...), custom_call_target="tpu_custom_call" | custom-call | tf_op jit(solution)/shard_map/band_pass/pallas_call | solution.py:952
  38.6 5.0 %place.1 = (bf16[96,192,128]{2,1,0:T(8,128)(2,1)}, bf16[256,128]{1,0:T(8,128)(2,1)}, f32[16,128]{1,0:T(8,128)}) custom-call(bf16[12,8,48,128]{3,2,1,0:T(8,128)(2,1)} %get-tuple-element.10.grads_ref, bf16[16,16,128]{2,1,0:T(8,128)(2,1)} %get-tuple-element.11.corner_ref, bf16[256,128]{1,0:T(8,128)(2,1)} %get-tuple-element.12.atom_ref, ...), custom_call_target="tpu_custom_call" | custom-call | tf_op jit(solution)/shard_map/place/pallas_call | solution.py:1125
